TPU v7x, 32 devices: a whole 2x2x4 slice. The times are simulated.
32 devices in a mesh: dp: 4 (over y, x), ctx: 8 (over z, core).
Axes of the slice: x: 2, y: 2, z: 4, core: 2. Of those that a mesh axis runs over, the one named last changes fastest.
Arguments:
- normed_layer_input: bfloat16 [4, 1024, 8192], P('dp', 'ctx'), may hold values from -6 to 6
- frozen_query_rows: bfloat16 [4, 1024, 2048], P('dp', 'ctx'), may hold values from -160 to 160
- projected_keys: bfloat16 [4, 1024, 256], P('dp', 'ctx'), may hold values from -7 to 7
- projected_values: bfloat16 [4, 1024, 256], P('dp', 'ctx'), may hold values from -6 to 6
- output_gradient: bfloat16 [4, 1024, 2048], P('dp', 'ctx'), may hold values from -6 to 6
- adapter_down: bfloat16 [8192, 16], replicated, may hold values from -0.0625 to 0.0625
- adapter_up: bfloat16 [16, 2048], replicated, may hold values from -1.5 to 1.5
- langevin_down_noise: float32 [8192, 16], replicated, may hold values from -1.8 to 1.8
- langevin_up_noise: float32 [16, 2048], replicated, may hold values from -0.6 to 0.6
- listed_key_blocks: int32 [16, 8, 12], replicated, may hold values from 0 to 7, as said below
- head_live_slots: int32 [16], replicated, may hold values from 4 to 12, as said below
Outputs:
- attention: bfloat16 [4, 1024, 2048], P('dp', 'ctx')
- step_down: float32 [8192, 16], replicated
- step_up: float32 [16, 2048], replicated
Inputs may be any that keep to these rules, and one draw needn't show every extreme that they name: `listed_key_blocks`: slot 0 of block b's list is b, slot 1 is b - 1, slot 2 is b + 1 (modulo 8), slot 3 is block 0, for every head; the other slots are any blocks. `head_live_slots`: each count is a multiple of 4.
All inputs are finite; a program needn't handle non-finite values.
Results may differ from a plain program's by a relative error of at most 0.013.
Values may be sent and summed in bfloat16 or wider, within the bound.
A program may use at most 128 MiB of HBM per device.

v0:
```python
import jax
import jax.numpy as jnp
from jax import lax
from jax.sharding import PartitionSpec as P

HEAD_SIZE = 128
G = 8
BLK = 128
NBMAX = 12


ADAPTER_GAIN = 2.0
MASK_VALUE = -1e30


def attention_weights(queries, key_rows, live_mask):
    scaling = queries.shape[-1] ** (-0.5)
    scores = (
        jnp.einsum("gqd,gkd->gqk", queries, key_rows, preferred_element_type=jnp.float32) * scaling
    )
    scores = jnp.where(live_mask[:, None, :], scores, MASK_VALUE)
    largest = jnp.max(scores, axis=-1, keepdims=True)
    shifted = jnp.exp(scores - largest)
    return shifted / jnp.sum(shifted, axis=-1, keepdims=True)


def forward_part(weights, value_rows):
    weights_low = weights.astype(jnp.bfloat16)
    return jnp.einsum(
        "gqk,gkd->gqd", weights_low, value_rows, preferred_element_type=jnp.float32
    ).astype(jnp.bfloat16)


def backward_part(weights, cotangent, key_rows, value_rows):
    scaling = key_rows.shape[-1] ** (-0.5)
    weight_grad = jnp.einsum(
        "gqd,gkd->gqk", cotangent, value_rows, preferred_element_type=jnp.float32
    )
    row_inner = jnp.sum(weights * weight_grad, axis=-1, keepdims=True)
    score_grad = (weights * (weight_grad - row_inner)).astype(jnp.bfloat16)
    return (
        jnp.einsum("gqk,gkd->gqd", score_grad, key_rows, preferred_element_type=jnp.float32)
        * scaling
    ).astype(jnp.bfloat16)


def both_parts(queries, cotangent, key_rows, value_rows, live_mask):
    weights = attention_weights(queries, key_rows, live_mask)
    return (
        forward_part(weights, value_rows),
        backward_part(weights, cotangent, key_rows, value_rows),
    )


def block_pass(
    work_fn, query_blocks, grad_blocks, key_blocks, value_blocks, slot_lists, live_mask, per_step
):
    block_total = query_blocks.shape[0]
    slot_count = slot_lists.shape[1]

    def grouped(tensor):
        return tensor.reshape((block_total // per_step, per_step) + tensor.shape[1:])

    def step_fn(pieces):
        query_part, grad_part, list_part, mask_part = pieces
        key_rows = key_blocks[list_part].reshape(per_step, slot_count * BLK, HEAD_SIZE)
        value_rows = value_blocks[list_part].reshape(per_step, slot_count * BLK, HEAD_SIZE)
        return work_fn(query_part, grad_part, key_rows, value_rows, mask_part)

    results = lax.map(
        step_fn,
        (grouped(query_blocks), grouped(grad_blocks), grouped(slot_lists), grouped(live_mask)),
    )
    return tuple((result.reshape(query_blocks.shape) for result in results))


def body(
    normed_layer_input,
    frozen_query_rows,
    projected_keys,
    projected_values,
    output_gradient,
    adapter_down,
    adapter_up,
    langevin_down_noise,
    langevin_up_noise,
    listed_key_blocks,
    head_live_slots,
):
    tok_rows = normed_layer_input.shape[1]
    head_total = frozen_query_rows.shape[2] // HEAD_SIZE
    group_total = projected_keys.shape[2] // HEAD_SIZE
    owners = lax.axis_size("ctx")
    reduced_rank_rows = jnp.dot(
        normed_layer_input[0], adapter_down, preferred_element_type=jnp.float32
    ).astype(jnp.bfloat16)
    query_matrix = (
        frozen_query_rows[0].astype(jnp.float32)
        + ADAPTER_GAIN * jnp.dot(reduced_rank_rows, adapter_up, preferred_element_type=jnp.float32)
    ).astype(jnp.bfloat16)
    query_cube = query_matrix.reshape(tok_rows, head_total, HEAD_SIZE)
    grad_cube = output_gradient[0].reshape(tok_rows, head_total, HEAD_SIZE)
    key_all, value_all = (
        lax.all_gather(projected_keys[0], "ctx", axis=0, tiled=True),
        lax.all_gather(projected_values[0], "ctx", axis=0, tiled=True),
    )
    block_total = key_all.shape[0] // BLK
    key_blocks = (
        key_all.reshape(block_total, BLK, group_total, HEAD_SIZE)
        .transpose(2, 0, 1, 3)
        .reshape(group_total * block_total, BLK, HEAD_SIZE)
    )
    value_blocks = (
        value_all.reshape(block_total, BLK, group_total, HEAD_SIZE)
        .transpose(2, 0, 1, 3)
        .reshape(group_total * block_total, BLK, HEAD_SIZE)
    )
    local_blocks = tok_rows // BLK
    first_block = lax.axis_index("ctx") * local_blocks
    local_lists = lax.dynamic_slice_in_dim(listed_key_blocks, first_block, local_blocks, 1)
    group_of = jnp.arange(head_total, dtype=jnp.int32) // G
    flat_lists = (local_lists + (group_of * block_total)[:, None, None]).reshape(
        head_total * local_blocks, NBMAX
    )
    query_blocks = (
        query_cube.reshape(local_blocks, BLK, head_total, HEAD_SIZE)
        .transpose(2, 0, 1, 3)
        .reshape(head_total * local_blocks, BLK, HEAD_SIZE)
    )
    grad_blocks = (
        grad_cube.reshape(local_blocks, BLK, head_total, HEAD_SIZE)
        .transpose(2, 0, 1, 3)
        .reshape(head_total * local_blocks, BLK, HEAD_SIZE)
    )
    live_rows = jnp.arange(NBMAX * BLK, dtype=jnp.int32)[None, :] // BLK < head_live_slots[:, None]
    live_mask = jnp.repeat(live_rows, local_blocks, axis=0)
    per_step = min(head_total * local_blocks, max(1, 512 // BLK))
    outputs, grads = block_pass(
        both_parts,
        query_blocks,
        grad_blocks,
        key_blocks,
        value_blocks,
        flat_lists,
        live_mask,
        per_step,
    )
    attended = (
        outputs.reshape(head_total, local_blocks, BLK, HEAD_SIZE)
        .transpose(1, 2, 0, 3)
        .reshape(tok_rows, head_total * HEAD_SIZE)
    )
    query_gradient = (
        grads.reshape(head_total, local_blocks, BLK, HEAD_SIZE)
        .transpose(1, 2, 0, 3)
        .reshape(tok_rows, head_total * HEAD_SIZE)
    )
    up_gradient = ADAPTER_GAIN * jnp.einsum(
        "tr,tc->rc", reduced_rank_rows, query_gradient, preferred_element_type=jnp.float32
    )
    reduced_gradient = (
        ADAPTER_GAIN
        * jnp.einsum("ns,ws->nw", query_gradient, adapter_up, preferred_element_type=jnp.float32)
    ).astype(jnp.bfloat16)
    grad_down = jnp.einsum(
        "td,tr->dr", normed_layer_input[0], reduced_gradient, preferred_element_type=jnp.float32
    )
    total_down, total_up = lax.psum((grad_down, up_gradient), ("dp", "ctx"))
    token_norm = (tok_rows * owners * lax.axis_size("dp")) ** (-0.5)
    return (
        attended[None],
        total_down * token_norm + langevin_down_noise,
        total_up * token_norm + langevin_up_noise,
    )


def solution(mesh):
    return jax.shard_map(
        body,
        mesh=mesh,
        in_specs=(
            P("dp", "ctx", None),
            P("dp", "ctx", None),
            P("dp", "ctx", None),
            P("dp", "ctx", None),
            P("dp", "ctx", None),
            P(),
            P(),
            P(),
            P(),
            P(),
            P(),
        ),
        out_specs=(P("dp", "ctx", None), P(), P()),
        check_vma=False,
    )
```

profile of v0, /device:TPU:0, one launch (start us, length us, event | category | flops | bytes accessed | tf_op | source)
XLA Modules:
  0.0 254.1 jit_solution(14525630807209720803)
XLA Ops:
  7.3 0.9 lt.34
  8.2 0.8 constant_dynamic-slice_fusion
  9.1 1.6 fusion.45
  10.7 0.3 fusion.43
  11.2 1.0 copy.27
  12.2 16.6 %all-gather = bf16[1,1024,256]{2,1,0:T(8,128)(2,1)S(1)} all-gather(bf16[1,128,256]{2,1,0:T(8,128)(2,1)S(1)} %copy-done.7), channel_id=2, replica_groups=mesh['dp'=4,'ctx'=8] {'ctx'}, dimensions={1}, use_global_device_ids=true | all-gather | bytes 589824 | tf_op jit(solution)/shard_map/all_gather | solution.py:104
  29.0 14.8 %all-gather.1 = bf16[1,1024,256]{2,1,0:T(8,128)(2,1)S(1)} all-gather(bf16[1,128,256]{2,1,0:T(8,128)(2,1)S(1)} %copy-done.8), channel_id=3, replica_groups=mesh['dp'=4,'ctx'=8] {'ctx'}, dimensions={1}, use_global_device_ids=true | all-gather | bytes 589824 | tf_op jit(solution)/shard_map/all_gather | solution.py:105
  43.7 0.9 reshape.128
  44.6 1.1 copy.30
  45.8 2.0 copy_bitcast_fusion
  48.0 60.9 %while.12 = (s32[]{:T(128)}, bf16[4,4,128,128]{3,2,1,0:T(8,128)(2,1)}, bf16[4,4,128,128]{2,3,1,0:T(8,128)(2,1)}, pred[4,4,1536]{2,1,0:T(4,128)(4,1)S(1)}, bf16[4...) while((s32[]{:T(128)}, ...), condition=%wide.region_4.5_spmd, body=%wide.region_0.4_spmd.sunk | while | flops 815728768 | bytes 57708056 | solution.py:70
  48.1 2.0 gather_fusion.1
  50.0 2.0 gather_fusion
  52.0 4.2 %fusion.84 = (f32[4,128]{1,0:T(4,128)S(1)}, f32[4,128,1536]{2,1,0:T(8,128)}) fusion(bf16[4,1536,128]{2,1,0:T(8,128)(2,1)} %bitcast.113, pred[4,1536]{1,0:T(4,128)(4,1)S(1)} %dynamic-slice_bitcast_fusion.2, bf16[4,4,128,128]{3,2,1,0:T(8,128)(2,1)} %get-tuple-element.164, s32[]{:T(128)S(6)} %copy.49), kind=kOutput, calls=%fused_computation.71.clone.1 | convolution fusion | flops 204473856 | bytes 4857860 | tf_op jit(solution)/shard_map/while/body/eval_jaxpr/sub | solution.py:23
  56.2 3.8 %fusion.85 = bf16[4,4,128,128]{3,2,1,0:T(8,128)(2,1)} fusion(bf16[4,4,128,128]{3,2,1,0:T(8,128)(2,1)} %get-tuple-element.151, s32[]{:T(128)S(6)} %copy.49, bf16[4,1536,128]{2,1,0:T(8,128)(2,1)} %bitcast.115, f32[4,128,1536]{2,1,0:T(8,128)} %get-tuple-element.136, f32[4,128]{1,0:T(4,128)S(1)} %get-tuple-element.137), kind=kOutput, calls=%fused_computation.18.clone.1 | convolution fusion | flops 202964992 | bytes 4851716 | tf_op jit(solution)/shard_map/while/body/eval_jaxpr/gqk,gkd->gqd/dot_general | solution.py:29
  60.0 1.7 multiply_reduce_fusion.2
  61.7 0.7 fusion.86
  62.4 0.1 copy.43
  62.5 0.7 constant_dynamic-update-slice_fusion.2
  63.3 2.0 gather_fusion.1
  65.3 2.0 gather_fusion
  67.2 4.2 %fusion.84 = (f32[4,128]{1,0:T(4,128)S(1)}, f32[4,128,1536]{2,1,0:T(8,128)}) fusion(bf16[4,1536,128]{2,1,0:T(8,128)(2,1)} %bitcast.113, pred[4,1536]{1,0:T(4,128)(4,1)S(1)} %dynamic-slice_bitcast_fusion.2, bf16[4,4,128,128]{3,2,1,0:T(8,128)(2,1)} %get-tuple-element.164, s32[]{:T(128)S(6)} %copy.49), kind=kOutput, calls=%fused_computation.71.clone.1 | convolution fusion | flops 204473856 | bytes 4857860 | tf_op jit(solution)/shard_map/while/body/eval_jaxpr/sub | solution.py:23
  71.4 3.8 %fusion.85 = bf16[4,4,128,128]{3,2,1,0:T(8,128)(2,1)} fusion(bf16[4,4,128,128]{3,2,1,0:T(8,128)(2,1)} %get-tuple-element.151, s32[]{:T(128)S(6)} %copy.49, bf16[4,1536,128]{2,1,0:T(8,128)(2,1)} %bitcast.115, f32[4,128,1536]{2,1,0:T(8,128)} %get-tuple-element.136, f32[4,128]{1,0:T(4,128)S(1)} %get-tuple-element.137), kind=kOutput, calls=%fused_computation.18.clone.1 | convolution fusion | flops 202964992 | bytes 4851716 | tf_op jit(solution)/shard_map/while/body/eval_jaxpr/gqk,gkd->gqd/dot_general | solution.py:29
  75.2 1.7 multiply_reduce_fusion.2
  76.9 0.7 fusion.86
  77.6 0.1 copy.43
  77.8 0.7 constant_dynamic-update-slice_fusion.2
  78.5 2.0 gather_fusion.1
  80.5 2.0 gather_fusion
  82.4 4.2 %fusion.84 = (f32[4,128]{1,0:T(4,128)S(1)}, f32[4,128,1536]{2,1,0:T(8,128)}) fusion(bf16[4,1536,128]{2,1,0:T(8,128)(2,1)} %bitcast.113, pred[4,1536]{1,0:T(4,128)(4,1)S(1)} %dynamic-slice_bitcast_fusion.2, bf16[4,4,128,128]{3,2,1,0:T(8,128)(2,1)} %get-tuple-element.164, s32[]{:T(128)S(6)} %copy.49), kind=kOutput, calls=%fused_computation.71.clone.1 | convolution fusion | flops 204473856 | bytes 4857860 | tf_op jit(solution)/shard_map/while/body/eval_jaxpr/sub | solution.py:23
  86.6 3.8 %fusion.85 = bf16[4,4,128,128]{3,2,1,0:T(8,128)(2,1)} fusion(bf16[4,4,128,128]{3,2,1,0:T(8,128)(2,1)} %get-tuple-element.151, s32[]{:T(128)S(6)} %copy.49, bf16[4,1536,128]{2,1,0:T(8,128)(2,1)} %bitcast.115, f32[4,128,1536]{2,1,0:T(8,128)} %get-tuple-element.136, f32[4,128]{1,0:T(4,128)S(1)} %get-tuple-element.137), kind=kOutput, calls=%fused_computation.18.clone.1 | convolution fusion | flops 202964992 | bytes 4851716 | tf_op jit(solution)/shard_map/while/body/eval_jaxpr/gqk,gkd->gqd/dot_general | solution.py:29
  90.4 1.7 multiply_reduce_fusion.2
  92.1 0.7 fusion.86
  93.0 0.7 constant_dynamic-update-slice_fusion.2
  93.8 2.0 gather_fusion.1
  95.7 2.0 gather_fusion
  97.7 4.2 %fusion.84 = (f32[4,128]{1,0:T(4,128)S(1)}, f32[4,128,1536]{2,1,0:T(8,128)}) fusion(bf16[4,1536,128]{2,1,0:T(8,128)(2,1)} %bitcast.113, pred[4,1536]{1,0:T(4,128)(4,1)S(1)} %dynamic-slice_bitcast_fusion.2, bf16[4,4,128,128]{3,2,1,0:T(8,128)(2,1)} %get-tuple-element.164, s32[]{:T(128)S(6)} %copy.49), kind=kOutput, calls=%fused_computation.71.clone.1 | convolution fusion | flops 204473856 | bytes 4857860 | tf_op jit(solution)/shard_map/while/body/eval_jaxpr/sub | solution.py:23
  101.8 3.8 %fusion.85 = bf16[4,4,128,128]{3,2,1,0:T(8,128)(2,1)} fusion(bf16[4,4,128,128]{3,2,1,0:T(8,128)(2,1)} %get-tuple-element.151, s32[]{:T(128)S(6)} %copy.49, bf16[4,1536,128]{2,1,0:T(8,128)(2,1)} %bitcast.115, f32[4,128,1536]{2,1,0:T(8,128)} %get-tuple-element.136, f32[4,128]{1,0:T(4,128)S(1)} %get-tuple-element.137), kind=kOutput, calls=%fused_computation.18.clone.1 | convolution fusion | flops 202964992 | bytes 4851716 | tf_op jit(solution)/shard_map/while/body/eval_jaxpr/gqk,gkd->gqd/dot_general | solution.py:29
  105.6 1.7 multiply_reduce_fusion.2
  107.4 0.7 fusion.86
  108.2 0.7 constant_dynamic-update-slice_fusion.2
  108.9 1.9 convolution_multiply_fusion.2
  110.8 2.4 convolution_bitcast_fusion
  113.3 1.4 copy.41
  114.7 1.0 broadcast_in_dim_reshape.3
  115.7 128.1 %all-reduce.3.cloned.1.call-done = (f32[8192,16]{0,1:T(8,128)}, f32[16,2048]{1,0:T(8,128)}) async-done(((f32[8192,16]{0,1:T(8,128)}, f32[16,2048]{1,0:T(8,128)}), (f32[8192,16]{0,1:T(8,128)}, f32[16,2048]{1,0:T(8,128)})) %all-reduce.3.cloned.1.call-update) | async-done | bytes 655376 | tf_op jit(solution)/shard_map/psum | solution.py:168
  243.8 1.9 multiply_add_fusion
  245.7 1.6 multiply_add_fusion.1
  (69 shorter events, 1.5 us)
Async XLA Ops:
  7.2 1.9 copy-start
  7.2 3.5 %copy-start.5 = (bf16[16,2048]{1,0:T(8,128)(2,1)S(1)}, bf16[16,2048]{1,0:T(8,128)(2,1)}, u32[]{:S(2)}) copy-start(bf16[16,2048]{1,0:T(8,128)(2,1)} %param.19) | copy-start | bytes 196612
  7.2 3.5 %copy-start.4 = (bf16[1,128,2048]{2,1,0:T(8,128)(2,1)S(1)}, bf16[1,128,2048]{2,1,0:T(8,128)(2,1)}, u32[]{:S(2)}) copy-start(bf16[1,128,2048]{2,1,0:T(8,128)(2,1)} %param.14) | copy-start | bytes 1572868
  7.2 236.6 %all-reduce.3.cloned.1.call-start = ((), (), s32[]{:S(2)}) async-start(), calls=%async_computation | async-start | bytes 1310720 | tf_op jit(solution)/shard_map/psum | solution.py:168
  10.7 1.5 copy-start.7
  11.2 17.8 %copy-start.8 = (bf16[1,128,256]{2,1,0:T(8,128)(2,1)S(1)}, bf16[1,128,256]{2,1,0:T(8,128)(2,1)}, u32[]{:S(2)}) copy-start(bf16[1,128,256]{2,1,0:T(8,128)(2,1)} %param.16) | copy-start | bytes 196612
  56.2 3.8 %copy-start.2 = (bf16[48,128,128]{2,1,0:T(8,128)(2,1)S(1)}, bf16[48,128,128]{2,1,0:T(8,128)(2,1)}, u32[]{:S(2)}) copy-start(bf16[48,128,128]{2,1,0:T(8,128)(2,1)} %gather_fusion) | copy-start | bytes 4718596 | tf_op jit(solution)/shard_map/while
  56.2 3.8 %copy-start.9 = (f32[4,128,1536]{2,1,0:T(8,128)S(1)}, f32[4,128,1536]{2,1,0:T(8,128)}, u32[]{:S(2)}) copy-start(f32[4,128,1536]{2,1,0:T(8,128)} %get-tuple-element.136) | copy-start | bytes 9437188 | tf_op jit(solution)/shard_map/while
  60.0 1.7 copy-start.1
  71.4 3.8 %copy-start.2 = (bf16[48,128,128]{2,1,0:T(8,128)(2,1)S(1)}, bf16[48,128,128]{2,1,0:T(8,128)(2,1)}, u32[]{:S(2)}) copy-start(bf16[48,128,128]{2,1,0:T(8,128)(2,1)} %gather_fusion) | copy-start | bytes 4718596 | tf_op jit(solution)/shard_map/while
  71.4 3.8 %copy-start.9 = (f32[4,128,1536]{2,1,0:T(8,128)S(1)}, f32[4,128,1536]{2,1,0:T(8,128)}, u32[]{:S(2)}) copy-start(f32[4,128,1536]{2,1,0:T(8,128)} %get-tuple-element.136) | copy-start | bytes 9437188 | tf_op jit(solution)/shard_map/while
  75.2 1.7 copy-start.1
  86.6 3.8 %copy-start.2 = (bf16[48,128,128]{2,1,0:T(8,128)(2,1)S(1)}, bf16[48,128,128]{2,1,0:T(8,128)(2,1)}, u32[]{:S(2)}) copy-start(bf16[48,128,128]{2,1,0:T(8,128)(2,1)} %gather_fusion) | copy-start | bytes 4718596 | tf_op jit(solution)/shard_map/while
  86.6 3.8 %copy-start.9 = (f32[4,128,1536]{2,1,0:T(8,128)S(1)}, f32[4,128,1536]{2,1,0:T(8,128)}, u32[]{:S(2)}) copy-start(f32[4,128,1536]{2,1,0:T(8,128)} %get-tuple-element.136) | copy-start | bytes 9437188 | tf_op jit(solution)/shard_map/while
  90.4 1.7 copy-start.1
  101.8 3.8 %copy-start.2 = (bf16[48,128,128]{2,1,0:T(8,128)(2,1)S(1)}, bf16[48,128,128]{2,1,0:T(8,128)(2,1)}, u32[]{:S(2)}) copy-start(bf16[48,128,128]{2,1,0:T(8,128)(2,1)} %gather_fusion) | copy-start | bytes 4718596 | tf_op jit(solution)/shard_map/while
  101.8 3.8 %copy-start.9 = (f32[4,128,1536]{2,1,0:T(8,128)S(1)}, f32[4,128,1536]{2,1,0:T(8,128)}, u32[]{:S(2)}) copy-start(f32[4,128,1536]{2,1,0:T(8,128)} %get-tuple-element.136) | copy-start | bytes 9437188 | tf_op jit(solution)/shard_map/while
  105.6 1.7 copy-start.1
  113.2 130.6 %copy-start.3 = (f32[8192,16]{0,1:T(8,128)S(1)}, f32[8192,16]{0,1:T(8,128)}, u32[]{:S(2)}) copy-start(f32[8192,16]{0,1:T(8,128)} %param.20) | copy-start | bytes 1572868
  113.2 132.5 %copy-start.6 = (f32[16,2048]{1,0:T(8,128)S(1)}, f32[16,2048]{1,0:T(8,128)}, u32[]{:S(2)}) copy-start(f32[16,2048]{1,0:T(8,128)} %param.21) | copy-start | bytes 393220
Sparse Core Ops, SparseCore 0:
  113.4 130.3 all-reduce.2
where the time goes:
time: 255 us; the launch traced here: 254 us
  waiting for transfers between devices  128 us (50%)
  matrix products  47.7 us (19%)
  blocking collectives  31.3 us (12%)
  local copies, waits for them, and re-layouts  28.9 us (11%)
  between operations  14.2 us (6%)
  other arithmetic  3.7 us (1%)
    psum x1, waiting for transfers between devices, body(): total_down, total_up = lax.psum((grad_down, up_gradient), ('dp', 'ctx'))  128 us
    sub x4, matrix products, attention_weights(): shifted = jnp.exp(scores - largest)  16.7 us
    all_gather x1, blocking collectives, body(): lax.all_gather(projected_keys[0], 'ctx', axis=0, tiled=True)  16.6 us
    dot_general x4, matrix products, forward_part(): jnp.einsum('gqk,gkd->gqd', weights_low, value_rows, preferred_element_typ...  15.2 us
    all_gather x1, blocking collectives, body(): lax.all_gather(projected_values[0], 'ctx', axis=0, tiled=True)  14.8 us
    gather x4, local copies, waits for them, and re-layouts, step_fn(): value_blocks[list_part].reshape(per_step, slot_count * BLK, HEAD_SIZE)  7.82 us
    gather x4, local copies, waits for them, and re-layouts, step_fn(): key_blocks[list_part].reshape(per_step, slot_count * BLK, HEAD_SIZE)  7.82 us
    dot_general x4, matrix products, backward_part(): jnp.einsum('gqd,gkd->gqk', cotangent, value_rows, preferred_element_type=...  6.83 us
  transfers between devices with their start and end apart: 1, of which 1 were waited for; matrix products, arithmetic and copies ran while one was open for 1% of the time, Pallas kernels for 0%

commit v1 on v0

v1 whole, which is shorter than its diff:
```python
import functools

import jax
import jax.numpy as jnp
from jax import lax
from jax.experimental import pallas as pl
from jax.experimental.pallas import tpu as pltpu
from jax.sharding import PartitionSpec as P

HEAD_SIZE = 128
G = 8
BLK = 128
ADAPTER_GAIN = 2.0
MASK_VALUE = -1e30
LOG2E = 1.4426950408889634
MESH = pl.DeviceIdType.MESH
F32 = jnp.float32
BF16 = jnp.bfloat16


def dot_nt(a, b):
    return lax.dot_general(a, b, (((1,), (1,)), ((), ())), preferred_element_type=F32)


def dot_tn(a, b):
    return lax.dot_general(a, b, (((0,), (0,)), ((), ())), preferred_element_type=F32)


def dot_nn(a, b):
    return jnp.dot(a, b, preferred_element_type=F32)


def kernel(
    ndp,
    nctx,
    per_step,
    x_hbm,
    frozen_hbm,
    k_hbm,
    v_hbm,
    og_hbm,
    down_t,
    up,
    lists,
    live,
    att_out,
    tot_down,
    tot_up,
    x,
    frozen,
    og,
    kv,
    q,
    qg,
    bias,
    gbuf,
    rbuf,
    zbuf,
    abuf,
    load_sem,
    z_send,
    z_recv,
    c_send,
    c_recv,
    rs_send,
    rs_recv,
    gz_send,
    gz_recv,
    ag_send,
    ag_recv,
):
    dp, ctx = lax.axis_index("dp"), lax.axis_index("ctx")
    nz, na = nctx // 2, ndp * 2
    z, core = lax.div(ctx, 2), lax.rem(ctx, 2)
    a = dp * 2 + core
    kvw = k_hbm.shape[1]
    width = x.shape[1]
    qw = q.shape[1]
    heads = qw // HEAD_SIZE
    wd, wu = width // na, qw // na
    keys = nctx * BLK

    def rows_of(c):
        return pl.ds(pl.multiple_of(c * BLK, BLK), BLK)

    def plane_id(k):
        p = lax.rem(a + k, na)
        return p, (lax.div(p, 2), z * 2 + lax.rem(p, 2))

    def line_id(k):
        return (dp, lax.rem(z + k, nz) * 2 + core)

    loads = []
    for i, (src, dst) in enumerate(
        (
            (k_hbm, kv.at[rows_of(ctx), pl.ds(0, kvw)]),
            (v_hbm, kv.at[rows_of(ctx), pl.ds(kvw, kvw)]),
            (x_hbm, x),
            (frozen_hbm, frozen),
            (og_hbm, og),
        )
    ):
        copy = pltpu.make_async_copy(src, dst, load_sem.at[i])
        copy.start()
        loads.append(copy)

    barrier = pltpu.get_barrier_semaphore()
    for k in range(1, na):
        pl.semaphore_signal(barrier, inc=1, device_id=plane_id(k)[1], device_id_type=MESH)
    for k in range(1, nz):
        pl.semaphore_signal(barrier, inc=1, device_id=line_id(k), device_id_type=MESH)
    pl.semaphore_wait(barrier, na - 1 + nz - 1)

    loads[0].wait()
    loads[1].wait()
    sibling = (dp, z * 2 + 1 - core)
    line_copies = []
    for k in range(1, nz):
        copy = pltpu.make_async_remote_copy(
            src_ref=kv.at[rows_of(ctx), :],
            dst_ref=kv.at[rows_of(ctx), :],
            send_sem=z_send.at[k],
            recv_sem=z_recv.at[k],
            device_id=line_id(k),
            device_id_type=MESH,
        )
        copy.start()
        line_copies.append(copy)

    def to_sibling(k):
        rows = rows_of(lax.rem(z - k + nz, nz) * 2 + core)
        copy = pltpu.make_async_remote_copy(
            src_ref=kv.at[rows, :],
            dst_ref=kv.at[rows, :],
            send_sem=c_send.at[k],
            recv_sem=c_recv.at[k],
            device_id=sibling,
            device_id_type=MESH,
        )
        copy.start()
        return copy

    core_copies = [to_sibling(0)]

    nqb, slots = lists.shape[1], lists.shape[2]
    mine = lax.broadcasted_iota(jnp.int32, lists.shape, 1) == ctx
    local = jnp.sum(jnp.where(mine, lists[...].astype(F32), 0.0), axis=1)
    head_iota = lax.broadcasted_iota(jnp.int32, (heads, 1), 0)
    live_col = jnp.zeros((heads, 1), jnp.int32)
    for h in range(heads):
        live_col = jnp.where(head_iota == h, live[h], live_col)
    slot_iota = lax.broadcasted_iota(jnp.int32, (heads, slots), 1)
    local = jnp.where(slot_iota < live_col, local, -1.0)
    block_of = (lax.broadcasted_iota(jnp.int32, (heads, keys), 1) // BLK).astype(F32)
    count = jnp.zeros((heads, keys), F32)
    for j in range(slots):
        count += jnp.where(block_of == local[:, j : j + 1], 1.0, 0.0)
    bias[...] = jnp.where(count > 0.0, jnp.log(jnp.maximum(count, 1.0)) * LOG2E, MASK_VALUE)

    loads[2].wait()
    low_rank = dot_nt(x[...], down_t[...]).astype(BF16)
    loads[3].wait()
    q[...] = (frozen[...].astype(F32) + ADAPTER_GAIN * dot_nn(low_rank, up[...])).astype(BF16)

    for k in range(1, nz):
        line_copies[k - 1].wait_recv()
        core_copies.append(to_sibling(k))
    for copy in core_copies:
        copy.wait_recv()
    loads[4].wait()

    scaling = HEAD_SIZE ** (-0.5)

    def one_head(h):
        group = h // G
        cols = pl.ds(pl.multiple_of(h * HEAD_SIZE, HEAD_SIZE), HEAD_SIZE)
        kcols = pl.ds(pl.multiple_of(group * HEAD_SIZE, HEAD_SIZE), HEAD_SIZE)
        vcols = pl.ds(pl.multiple_of(kvw + group * HEAD_SIZE, HEAD_SIZE), HEAD_SIZE)
        key_rows, value_rows = kv[:, kcols], kv[:, vcols]
        scores = dot_nt(q[:, cols], key_rows) * (scaling * LOG2E) + bias[pl.ds(h, 1), :]
        weights = jnp.exp2(scores - jnp.max(scores, axis=-1, keepdims=True))
        weight_grad = dot_nt(og[:, cols], value_rows)
        inverse = 1.0 / jnp.sum(weights, axis=-1, keepdims=True)
        inner = jnp.sum(weights * weight_grad, axis=-1, keepdims=True) * inverse
        score_grad = (weights * (weight_grad - inner)).astype(BF16)
        att_out[:, cols] = (dot_nn(weights.astype(BF16), value_rows) * inverse).astype(BF16)
        qg[:, cols] = (dot_nn(score_grad, key_rows) * (inverse * scaling)).astype(BF16)

    def head_step(i, carry):
        for j in range(per_step):
            one_head(i * per_step + j)
        return carry

    lax.fori_loop(0, heads // per_step, head_step, 0)

    low_grad = (ADAPTER_GAIN * dot_nt(qg[...], up[...])).astype(BF16)

    def chunk(p):
        dcols = pl.ds(pl.multiple_of(p * wd, 128), wd)
        ucols = pl.ds(pl.multiple_of(p * wu, 128), wu)
        return dot_tn(low_grad, x[:, dcols]), ADAPTER_GAIN * dot_tn(low_rank, qg[:, ucols])

    rs_copies = []
    for k in range(1, na):
        p, device = plane_id(k)
        part_down, part_up = chunk(p)
        gbuf[k, :, :wd] = part_down.astype(BF16)
        gbuf[k, :, wd:] = part_up.astype(BF16)
        copy = pltpu.make_async_remote_copy(
            src_ref=gbuf.at[k],
            dst_ref=rbuf.at[k],
            send_sem=rs_send.at[k],
            recv_sem=rs_recv.at[k],
            device_id=device,
            device_id_type=MESH,
        )
        copy.start()
        rs_copies.append(copy)
    sum_down, sum_up = chunk(a)
    for k in range(1, na):
        rs_copies[k - 1].wait_recv()
        sum_down += rbuf[k, :, :wd].astype(F32)
        sum_up += rbuf[k, :, wd:].astype(F32)
    zbuf[z, :, :wd] = sum_down.astype(BF16)
    zbuf[z, :, wd:] = sum_up.astype(BF16)

    gz_copies = []
    for k in range(1, nz):
        copy = pltpu.make_async_remote_copy(
            src_ref=zbuf.at[z],
            dst_ref=zbuf.at[z],
            send_sem=gz_send.at[k],
            recv_sem=gz_recv.at[k],
            device_id=line_id(k),
            device_id_type=MESH,
        )
        copy.start()
        gz_copies.append(copy)
    for copy in gz_copies:
        copy.wait_recv()
    total = zbuf[0].astype(F32)
    for i in range(1, nz):
        total += zbuf[i].astype(F32)
    abuf[a] = total.astype(BF16)

    ag_copies = []
    for k in range(1, na):
        copy = pltpu.make_async_remote_copy(
            src_ref=abuf.at[a],
            dst_ref=abuf.at[a],
            send_sem=ag_send.at[k],
            recv_sem=ag_recv.at[k],
            device_id=plane_id(k)[1],
            device_id_type=MESH,
        )
        copy.start()
        ag_copies.append(copy)
    for copy in line_copies + core_copies + rs_copies + gz_copies:
        copy.wait_send()
    for copy in ag_copies:
        copy.wait()
    for p in range(na):
        tot_down[:, p * wd : (p + 1) * wd] = abuf[p, :, :wd]
        tot_up[:, p * wu : (p + 1) * wu] = abuf[p, :, wd:]


def body(
    ndp,
    nctx,
    normed_layer_input,
    frozen_query_rows,
    projected_keys,
    projected_values,
    output_gradient,
    adapter_down,
    adapter_up,
    langevin_down_noise,
    langevin_up_noise,
    listed_key_blocks,
    head_live_slots,
):
    tok, width = normed_layer_input.shape[1:]
    qw, kvw = frozen_query_rows.shape[2], projected_keys.shape[2]
    rank = adapter_up.shape[0]
    heads = qw // HEAD_SIZE
    keys = nctx * tok
    nz, na = nctx // 2, ndp * 2
    piece = (width + qw) // na
    per_step = 2 if keys <= 1024 else 1
    any_spec = pl.BlockSpec(memory_space=pl.ANY)
    vmem_spec = pl.BlockSpec(memory_space=pltpu.VMEM)
    smem_spec = pl.BlockSpec(memory_space=pltpu.SMEM)
    dma = pltpu.SemaphoreType.DMA
    attended, total_down, total_up = pl.pallas_call(
        functools.partial(kernel, ndp, nctx, per_step),
        out_shape=(
            jax.ShapeDtypeStruct((tok, qw), BF16),
            jax.ShapeDtypeStruct((rank, width), BF16),
            jax.ShapeDtypeStruct((rank, qw), BF16),
        ),
        in_specs=[any_spec] * 5 + [vmem_spec] * 3 + [smem_spec],
        out_specs=(vmem_spec, vmem_spec, vmem_spec),
        scratch_shapes=[
            pltpu.VMEM((tok, width), BF16),
            pltpu.VMEM((tok, qw), BF16),
            pltpu.VMEM((tok, qw), BF16),
            pltpu.VMEM((keys, 2 * kvw), BF16),
            pltpu.VMEM((tok, qw), BF16),
            pltpu.VMEM((tok, qw), BF16),
            pltpu.VMEM((heads, keys), F32),
            pltpu.VMEM((na, rank, piece), BF16),
            pltpu.VMEM((na, rank, piece), BF16),
            pltpu.VMEM((nz, rank, piece), BF16),
            pltpu.VMEM((na, rank, piece), BF16),
            dma((5,)),
            dma((nz,)),
            dma((nz,)),
            dma((nz,)),
            dma((nz,)),
            dma((na,)),
            dma((na,)),
            dma((nz,)),
            dma((nz,)),
            dma((na,)),
            dma((na,)),
        ],
        compiler_params=pltpu.CompilerParams(
            collective_id=0, has_side_effects=True, vmem_limit_bytes=56 * 2**20
        ),
        name="adapter_attention",
    )(
        normed_layer_input[0],
        frozen_query_rows[0],
        projected_keys[0],
        projected_values[0],
        output_gradient[0],
        adapter_down.T,
        adapter_up,
        listed_key_blocks,
        head_live_slots,
    )
    token_norm = (tok * nctx * ndp) ** (-0.5)
    return (
        attended[None],
        total_down.T.astype(F32) * token_norm + langevin_down_noise,
        total_up.astype(F32) * token_norm + langevin_up_noise,
    )


def solution(mesh):
    rows = P("dp", "ctx", None)
    return jax.shard_map(
        functools.partial(body, mesh.shape["dp"], mesh.shape["ctx"]),
        mesh=mesh,
        in_specs=(rows,) * 5 + (P(),) * 6,
        out_specs=(rows, P(), P()),
        check_vma=False,
    )
```

time: 255 us -> 54 us (0.21)
  waiting for transfers between devices: 128 us -> 0 us
  matrix products: 47.7 us -> 0 us
  Pallas kernels: 0 us -> 46.3 us
  blocking collectives: 31.3 us -> 0 us
  local copies, waits for them, and re-layouts: 28.9 us -> 3.49 us
  between operations: 14.2 us -> 0.66 us
    psum x1 -> x0, waiting for transfers between devices: 128 us -> none  [body(): total_down, total_up = lax.psum((grad_down, up_gradient), ('dp', 'ctx'))]
    pallas_call x0 -> x1, Pallas kernels: none -> 46.3 us  [body(): pl.pallas_call(functools.partial(kernel, ndp, nctx, per_step), out_shape=...]
    all_gather x2 -> x0, blocking collectives: 31.3 us -> none  [the longest x1 16.6 us: body(): lax.all_gather(projected_keys[0], 'ctx', axis=0, tiled=True)]
    dot_general x16 -> x0, matrix products: 31 us -> none  [the longest x4 15.2 us: forward_part(): jnp.einsum('gqk,gkd->gqd', weights_low, value_rows, preferred_element_typ...]
    sub x4 -> x0, matrix products: 16.7 us -> none  [attention_weights(): shifted = jnp.exp(scores - largest)]
    gather x8 -> x0, local copies, waits for them, and re-layouts: 15.6 us -> none  [the longest x4 7.82 us: step_fn(): value_blocks[list_part].reshape(per_step, slot_count * BLK, HEAD_SIZE)]
    another operation x3 -> x0, local copies, waits for them, and re-layouts: 4.45 us -> none  [the longest x1 1.99 us: body(): grad_cube.reshape(local_blocks, BLK, head_total, HEAD_SIZE)]
    unnamed x16 -> x6, local copies, waits for them, and re-layouts: 0.24 us -> 3.49 us
  transfers between devices with their start and end apart: 1 -> 0, of which waited for: 1 -> 0; matrix products, arithmetic and copies ran while one was open for 1% -> 0% of each run, Pallas kernels for 0% -> 0%
where the time goes in v1:
time: 54 us; the launch traced here: 53.7 us
  Pallas kernels  46.3 us (86%)
  local copies, waits for them, and re-layouts  3.49 us (6%)
  other arithmetic  3.31 us (6%)
  between operations  0.66 us (1%)
    pallas_call x1, Pallas kernels, body(): pl.pallas_call(functools.partial(kernel, ndp, nctx, per_step), out_shape=...  46.3 us
    unnamed x6, local copies, waits for them, and re-layouts  3.49 us
    add x1, other arithmetic, body(): total_down.T.astype(F32) * token_norm + langevin_down_noise  1.8 us
    add x1, other arithmetic, body(): total_up.astype(F32) * token_norm + langevin_up_noise  1.51 us

profile of v1, /device:TPU:0, one launch (start us, length us, event | category | flops | bytes accessed | tf_op | source)
XLA Modules:
  0.0 53.7 jit_solution(2478541383149307333)
XLA Ops:
  0.6 0.0 copy-start
  0.6 1.6 %copy.14.lists = s32[16,8,12]{2,1,0:T(8,128)} copy(s32[16,8,12]{0,1,2:T(8,128)} %param.20) | data formatting | bytes 12288 | tf_op args[9]
  2.2 0.0 copy-start.1
  2.2 46.3 %adapter_attention.1 = (bf16[128,2048]{1,0:T(8,128)(2,1)}, bf16[16,8192]{1,0:T(8,128)(2,1)}, bf16[16,2048]{1,0:T(8,128)(2,1)}) custom-call(bf16[128,8192]{1,0:T(8,128)(2,1)} %bitcast.9, bf16[128,2048]{1,0:T(8,128)(2,1)} %bitcast.11, bf16[128,256]{1,0:T(8,128)(2,1)} %bitcast.14, bf16[128,256]{1,0:T(8,128)(2,1)} %bitcast.15, bf16[128,2048]{1,0:T(8,128)(2,1)} %bitcast.12, ...), custom_call_target="tpu_custom_call" | custom-call | tf_op jit(solution)/shard_map/adapter_attention/pallas_call | solution.py:294
  48.5 0.0 copy-done
  48.6 1.8 %bitcast_add_fusion = f32[8192,16]{0,1:T(8,128)} fusion(f32[8192,16]{0,1:T(8,128)S(1)} %copy-done, bf16[16,8192]{1,0:T(8,128)(2,1)} %get-tuple-element.7), kind=kLoop, calls=%fused_computation | loop fusion | flops 393216 | bytes 1310720 | tf_op jit(solution)/shard_map/add | solution.py:345
  50.4 0.0 copy-done.1
  50.4 1.5 %multiply_add_fusion = f32[16,2048]{1,0:T(8,128)} fusion(f32[16,2048]{1,0:T(8,128)S(1)} %copy-done.1, bf16[16,2048]{1,0:T(8,128)(2,1)} %get-tuple-element.8), kind=kLoop, calls=%fused_computation.1 | loop fusion | flops 98304 | bytes 327680 | tf_op jit(solution)/shard_map/add | solution.py:346
  51.9 1.9 %copy.16 = bf16[1,128,2048]{2,1,0:T(8,128)(2,1)} copy(bf16[1,128,2048]{2,1,0:T(8,128)(2,1)} %bitcast.10) | data formatting | bytes 1048576
Async XLA Ops:
  0.6 47.9 %copy-start = (f32[8192,16]{0,1:T(8,128)S(1)}, f32[8192,16]{0,1:T(8,128)}, u32[]{:S(2)}) copy-start(f32[8192,16]{0,1:T(8,128)} %param.18) | copy-start | bytes 1572868
  2.2 48.1 %copy-start.1 = (f32[16,2048]{1,0:T(8,128)S(1)}, f32[16,2048]{1,0:T(8,128)}, u32[]{:S(2)}) copy-start(f32[16,2048]{1,0:T(8,128)} %param.19) | copy-start | bytes 393220

commit v2 on v1

--- a/solution.py
+++ b/solution.py
@@ -34,30 +34,39 @@
     ndp,
     nctx,
     per_step,
+    early,
     x_hbm,
     frozen_hbm,
     k_hbm,
     v_hbm,
     og_hbm,
+    noise_down_hbm,
+    noise_up_hbm,
     down_t,
     up,
     lists,
     live,
-    att_out,
-    tot_down,
-    tot_up,
+    att_hbm,
+    step_down_hbm,
+    step_up_hbm,
     x,
     frozen,
     og,
     kv,
     q,
     qg,
+    att,
+    step_down,
+    step_up,
     bias,
+    scores_buf,
+    grads_buf,
     gbuf,
     rbuf,
     zbuf,
     abuf,
     load_sem,
+    store_sem,
     z_send,
     z_recv,
     c_send,
@@ -80,24 +89,36 @@
     wd, wu = width // na, qw // na
     keys = nctx * BLK
 
-    def rows_of(c):
-        return pl.ds(pl.multiple_of(c * BLK, BLK), BLK)
+    own_rows = pl.ds(pl.multiple_of(core * BLK, BLK), BLK)
+
+    def line(k):
+        if nz & (nz - 1):
+            return lax.rem(z + nz - k, nz)
+        other, bit = z, 1
+        while bit < nz:
+            if k & bit:
+                other = other + bit * (1 - 2 * lax.rem(lax.div(z, bit), 2))
+            bit *= 2
+        return other
 
     def plane_id(k):
         p = lax.rem(a + k, na)
         return p, (lax.div(p, 2), z * 2 + lax.rem(p, 2))
 
     def line_id(k):
-        return (dp, lax.rem(z + k, nz) * 2 + core)
+        to = lax.rem(z + k, nz) if nz & (nz - 1) else line(k)
+        return (dp, to * 2 + core)
 
     loads = []
     for i, (src, dst) in enumerate(
         (
-            (k_hbm, kv.at[rows_of(ctx), pl.ds(0, kvw)]),
-            (v_hbm, kv.at[rows_of(ctx), pl.ds(kvw, kvw)]),
+            (k_hbm, kv.at[0, own_rows, pl.ds(0, kvw)]),
+            (v_hbm, kv.at[0, own_rows, pl.ds(kvw, kvw)]),
             (x_hbm, x),
             (frozen_hbm, frozen),
             (og_hbm, og),
+            (noise_down_hbm, step_down),
+            (noise_up_hbm, step_up),
         )
     ):
         copy = pltpu.make_async_copy(src, dst, load_sem.at[i])
@@ -117,8 +138,8 @@
     line_copies = []
     for k in range(1, nz):
         copy = pltpu.make_async_remote_copy(
-            src_ref=kv.at[rows_of(ctx), :],
-            dst_ref=kv.at[rows_of(ctx), :],
+            src_ref=kv.at[0, own_rows, :],
+            dst_ref=kv.at[k, own_rows, :],
             send_sem=z_send.at[k],
             recv_sem=z_recv.at[k],
             device_id=line_id(k),
@@ -128,10 +149,9 @@
         line_copies.append(copy)
 
     def to_sibling(k):
-        rows = rows_of(lax.rem(z - k + nz, nz) * 2 + core)
         copy = pltpu.make_async_remote_copy(
-            src_ref=kv.at[rows, :],
-            dst_ref=kv.at[rows, :],
+            src_ref=kv.at[k, own_rows, :],
+            dst_ref=kv.at[k, own_rows, :],
             send_sem=c_send.at[k],
             recv_sem=c_recv.at[k],
             device_id=sibling,
@@ -142,56 +162,104 @@
 
     core_copies = [to_sibling(0)]
 
-    nqb, slots = lists.shape[1], lists.shape[2]
+    slots, nqb = lists.shape[:2]
     mine = lax.broadcasted_iota(jnp.int32, lists.shape, 1) == ctx
     local = jnp.sum(jnp.where(mine, lists[...].astype(F32), 0.0), axis=1)
-    head_iota = lax.broadcasted_iota(jnp.int32, (heads, 1), 0)
-    live_col = jnp.zeros((heads, 1), jnp.int32)
+    head_iota = lax.broadcasted_iota(jnp.int32, (1, heads), 1)
+    live_row = jnp.zeros((1, heads), jnp.int32)
     for h in range(heads):
-        live_col = jnp.where(head_iota == h, live[h], live_col)
-    slot_iota = lax.broadcasted_iota(jnp.int32, (heads, slots), 1)
-    local = jnp.where(slot_iota < live_col, local, -1.0)
-    block_of = (lax.broadcasted_iota(jnp.int32, (heads, keys), 1) // BLK).astype(F32)
-    count = jnp.zeros((heads, keys), F32)
+        live_row = jnp.where(head_iota == h, live[h], live_row)
+    block_iota = lax.broadcasted_iota(jnp.int32, (nqb, heads), 0).astype(F32)
+    count = jnp.zeros((nqb, heads), F32)
     for j in range(slots):
-        count += jnp.where(block_of == local[:, j : j + 1], 1.0, 0.0)
-    bias[...] = jnp.where(count > 0.0, jnp.log(jnp.maximum(count, 1.0)) * LOG2E, MASK_VALUE)
+        listed = jnp.where(live_row > j, local[j : j + 1, :], -1.0)
+        count += jnp.where(block_iota == listed, 1.0, 0.0)
+    lane = lax.broadcasted_iota(jnp.int32, (1, keys), 1)
+    held = jnp.zeros((1, keys), jnp.int32)
+    for k in range(nz):
+        held = jnp.where(lane // (2 * BLK) == k, line(k) * 2, held)
+    held += (lane // BLK) % 2
+    spread = jnp.where(lax.broadcasted_iota(jnp.int32, (nqb, keys), 0) == held, 1.0, 0.0)
+    count = dot_tn(count, spread)
+    bias[...] = jnp.where(count > 0.5, jnp.log(jnp.maximum(count, 1.0)) * LOG2E, MASK_VALUE)
 
     loads[2].wait()
     low_rank = dot_nt(x[...], down_t[...]).astype(BF16)
     loads[3].wait()
     q[...] = (frozen[...].astype(F32) + ADAPTER_GAIN * dot_nn(low_rank, up[...])).astype(BF16)
 
-    for k in range(1, nz):
-        line_copies[k - 1].wait_recv()
-        core_copies.append(to_sibling(k))
-    for copy in core_copies:
-        copy.wait_recv()
     loads[4].wait()
-
     scaling = HEAD_SIZE ** (-0.5)
-
-    def one_head(h):
-        group = h // G
-        cols = pl.ds(pl.multiple_of(h * HEAD_SIZE, HEAD_SIZE), HEAD_SIZE)
+    pair = 2 * BLK
+
+    def stacked(ref, first, number):
+        return jnp.concatenate(
+            [
+                ref[:, pl.ds(pl.multiple_of((first + j) * HEAD_SIZE, HEAD_SIZE), HEAD_SIZE)]
+                for j in range(number)
+            ],
+            axis=0,
+        )
+
+    def scores_of(k):
+        def group_step(group, carry):
+            kcols = pl.ds(pl.multiple_of(group * HEAD_SIZE, HEAD_SIZE), HEAD_SIZE)
+            vcols = pl.ds(pl.multiple_of(kvw + group * HEAD_SIZE, HEAD_SIZE), HEAD_SIZE)
+            rows = pl.ds(pl.multiple_of(group * G * BLK, G * BLK), G * BLK)
+            scores_buf[k, rows, :] = dot_nt(stacked(q, group * G, G), kv[k, :, kcols])
+            grads_buf[k, rows, :] = dot_nt(stacked(og, group * G, G), kv[k, :, vcols])
+            return carry
+
+        lax.fori_loop(0, heads // G, group_step, 0)
+
+    for k in range(nz):
+        if k > 0:
+            line_copies[k - 1].wait_recv()
+            core_copies.append(to_sibling(k))
+        if early:
+            core_copies[k].wait_recv()
+            scores_of(k)
+    if not early:
+        for copy in core_copies:
+            copy.wait_recv()
+
+    def head_step(i, carry):
+        first = i * per_step
+        group = first // G
         kcols = pl.ds(pl.multiple_of(group * HEAD_SIZE, HEAD_SIZE), HEAD_SIZE)
         vcols = pl.ds(pl.multiple_of(kvw + group * HEAD_SIZE, HEAD_SIZE), HEAD_SIZE)
-        key_rows, value_rows = kv[:, kcols], kv[:, vcols]
-        scores = dot_nt(q[:, cols], key_rows) * (scaling * LOG2E) + bias[pl.ds(h, 1), :]
-        weights = jnp.exp2(scores - jnp.max(scores, axis=-1, keepdims=True))
-        weight_grad = dot_nt(og[:, cols], value_rows)
-        inverse = 1.0 / jnp.sum(weights, axis=-1, keepdims=True)
-        inner = jnp.sum(weights * weight_grad, axis=-1, keepdims=True) * inverse
-        score_grad = (weights * (weight_grad - inner)).astype(BF16)
-        att_out[:, cols] = (dot_nn(weights.astype(BF16), value_rows) * inverse).astype(BF16)
-        qg[:, cols] = (dot_nn(score_grad, key_rows) * (inverse * scaling)).astype(BF16)
-
-    def head_step(i, carry):
+        key_rows = kv[:, :, kcols].reshape(keys, HEAD_SIZE)
+        value_rows = kv[:, :, vcols].reshape(keys, HEAD_SIZE)
+        all_weights, all_grads, all_inverse = [], [], []
         for j in range(per_step):
-            one_head(i * per_step + j)
+            h = first + j
+            if early:
+                rows = pl.ds(pl.multiple_of(h * BLK, BLK), BLK)
+                scores = jnp.concatenate([scores_buf[k, rows, :] for k in range(nz)], axis=1)
+                weight_grad = jnp.concatenate([grads_buf[k, rows, :] for k in range(nz)], axis=1)
+            else:
+                cols = pl.ds(pl.multiple_of(h * HEAD_SIZE, HEAD_SIZE), HEAD_SIZE)
+                scores = dot_nt(q[:, cols], key_rows)
+                weight_grad = dot_nt(og[:, cols], value_rows)
+            scores = scores * (scaling * LOG2E) + bias[pl.ds(h, 1), :]
+            weights = jnp.exp2(scores - jnp.max(scores, axis=-1, keepdims=True))
+            inverse = 1.0 / jnp.sum(weights, axis=-1, keepdims=True)
+            inner = jnp.sum(weights * weight_grad, axis=-1, keepdims=True) * inverse
+            all_weights.append(weights.astype(BF16))
+            all_grads.append((weights * (weight_grad - inner)).astype(BF16))
+            all_inverse.append(inverse)
+        attended = dot_nn(jnp.concatenate(all_weights, axis=0), value_rows)
+        query_grad = dot_nn(jnp.concatenate(all_grads, axis=0), key_rows)
+        for j in range(per_step):
+            cols = pl.ds(pl.multiple_of((first + j) * HEAD_SIZE, HEAD_SIZE), HEAD_SIZE)
+            rows = slice(j * BLK, (j + 1) * BLK)
+            att[:, cols] = (attended[rows] * all_inverse[j]).astype(BF16)
+            qg[:, cols] = (query_grad[rows] * (all_inverse[j] * scaling)).astype(BF16)
         return carry
 
     lax.fori_loop(0, heads // per_step, head_step, 0)
+    att_store = pltpu.make_async_copy(att, att_hbm, store_sem.at[0])
+    att_store.start()
 
     low_grad = (ADAPTER_GAIN * dot_nt(qg[...], up[...])).astype(BF16)
 
@@ -257,11 +325,38 @@
         ag_copies.append(copy)
     for copy in line_copies + core_copies + rs_copies + gz_copies:
         copy.wait_send()
+    loads[5].wait()
+    loads[6].wait()
     for copy in ag_copies:
         copy.wait()
+    norm = (BLK * nctx * ndp) ** (-0.5)
     for p in range(na):
-        tot_down[:, p * wd : (p + 1) * wd] = abuf[p, :, :wd]
-        tot_up[:, p * wu : (p + 1) * wu] = abuf[p, :, wd:]
+        step_down[:, p * wd : (p + 1) * wd] += abuf[p, :, :wd].astype(F32) * norm
+        step_up[:, p * wu : (p + 1) * wu] += abuf[p, :, wd:].astype(F32) * norm
+    stores = [
+        pltpu.make_async_copy(step_down, step_down_hbm, store_sem.at[1]),
+        pltpu.make_async_copy(step_up, step_up_hbm, store_sem.at[2]),
+    ]
+    for copy in stores:
+        copy.start()
+    for copy in [att_store] + stores:
+        copy.wait()
+
+
+def hand_over(*refs):
+    sem = refs[-1]
+    copies = []
+    for i in range(3):
+        rows = refs[i].shape[0] // 2
+        for j in range(2):
+            part = pl.ds(j * rows, rows)
+            copies.append(
+                pltpu.make_async_copy(refs[i].at[part], refs[3 + i].at[part], sem.at[2 * i + j])
+            )
+    for copy in copies:
+        copy.start()
+    for copy in copies:
+        copy.wait()
 
 
 def body(
@@ -286,33 +381,42 @@
     keys = nctx * tok
     nz, na = nctx // 2, ndp * 2
     piece = (width + qw) // na
-    per_step = 2 if keys <= 1024 else 1
+    early = 2 * heads * tok * keys * 4 <= 2**24
+    per_step = 4 if early else 1
     any_spec = pl.BlockSpec(memory_space=pl.ANY)
     vmem_spec = pl.BlockSpec(memory_space=pltpu.VMEM)
     smem_spec = pl.BlockSpec(memory_space=pltpu.SMEM)
     dma = pltpu.SemaphoreType.DMA
-    attended, total_down, total_up = pl.pallas_call(
-        functools.partial(kernel, ndp, nctx, per_step),
-        out_shape=(
-            jax.ShapeDtypeStruct((tok, qw), BF16),
-            jax.ShapeDtypeStruct((rank, width), BF16),
-            jax.ShapeDtypeStruct((rank, qw), BF16),
-        ),
-        in_specs=[any_spec] * 5 + [vmem_spec] * 3 + [smem_spec],
-        out_specs=(vmem_spec, vmem_spec, vmem_spec),
+    held_scores = (nz, heads * tok, 2 * BLK) if early else (1, 8, 128)
+    results = (
+        jax.ShapeDtypeStruct((tok, qw), BF16),
+        jax.ShapeDtypeStruct((rank, width), F32),
+        jax.ShapeDtypeStruct((rank, qw), F32),
+    )
+    outputs = pl.pallas_call(
+        functools.partial(kernel, ndp, nctx, per_step, early),
+        out_shape=results,
+        in_specs=[any_spec] * 7 + [vmem_spec] * 3 + [smem_spec],
+        out_specs=(any_spec,) * 3,
         scratch_shapes=[
             pltpu.VMEM((tok, width), BF16),
             pltpu.VMEM((tok, qw), BF16),
             pltpu.VMEM((tok, qw), BF16),
-            pltpu.VMEM((keys, 2 * kvw), BF16),
+            pltpu.VMEM((nz, 2 * BLK, 2 * kvw), BF16),
             pltpu.VMEM((tok, qw), BF16),
             pltpu.VMEM((tok, qw), BF16),
+            pltpu.VMEM((tok, qw), BF16),
+            pltpu.VMEM((rank, width), F32),
+            pltpu.VMEM((rank, qw), F32),
             pltpu.VMEM((heads, keys), F32),
+            pltpu.VMEM(held_scores, F32),
+            pltpu.VMEM(held_scores, F32),
             pltpu.VMEM((na, rank, piece), BF16),
             pltpu.VMEM((na, rank, piece), BF16),
             pltpu.VMEM((nz, rank, piece), BF16),
             pltpu.VMEM((na, rank, piece), BF16),
-            dma((5,)),
+            dma((7,)),
+            dma((3,)),
             dma((nz,)),
             dma((nz,)),
             dma((nz,)),
@@ -325,7 +429,9 @@
             dma((na,)),
         ],
         compiler_params=pltpu.CompilerParams(
-            collective_id=0, has_side_effects=True, vmem_limit_bytes=56 * 2**20
+            collective_id=0,
+            has_side_effects=True,
+            vmem_limit_bytes=60 * 2**20,
         ),
         name="adapter_attention",
     )(
@@ -334,17 +440,22 @@
         projected_keys[0],
         projected_values[0],
         output_gradient[0],
+        langevin_down_noise.T,
+        langevin_up_noise,
         adapter_down.T,
         adapter_up,
-        listed_key_blocks,
+        listed_key_blocks.transpose(2, 1, 0),
         head_live_slots,
     )
-    token_norm = (tok * nctx * ndp) ** (-0.5)
-    return (
-        attended[None],
-        total_down.T.astype(F32) * token_norm + langevin_down_noise,
-        total_up.astype(F32) * token_norm + langevin_up_noise,
-    )
+    attended, step_down, step_up = pl.pallas_call(
+        hand_over,
+        out_shape=results,
+        in_specs=[any_spec] * 3,
+        out_specs=(any_spec,) * 3,
+        scratch_shapes=[dma((6,))],
+        name="hand_over",
+    )(*outputs)
+    return attended[None], step_down.T, step_up
 
 
 def solution(mesh):

time: 54 us -> 82.2 us (1.52)
  Pallas kernels: 46.3 us -> 81.4 us
  local copies, waits for them, and re-layouts: 3.49 us -> 0 us
  other arithmetic: 3.31 us -> 0 us
    pallas_call x1 -> x2, Pallas kernels: 46.3 us -> 81.4 us  [the longest x1 44.5 us: body(): pl.pallas_call(functools.partial(kernel, ndp, nctx, per_step, early), out...]
    unnamed x6 -> x0, local copies, waits for them, and re-layouts: 3.49 us -> none
    add x2 -> x0, other arithmetic: 3.31 us -> none  [the longest x1 1.8 us: body(): total_down.T.astype(F32) * token_norm + langevin_down_noise]
where the time goes in v2:
time: 82.2 us; the launch traced here: 82 us
  Pallas kernels  81.4 us (99%)
    pallas_call x1, Pallas kernels, body(): pl.pallas_call(functools.partial(kernel, ndp, nctx, per_step, early), out...  44.5 us
    pallas_call x1, Pallas kernels, body(): pl.pallas_call(hand_over, out_shape=results, in_specs=[any_spec] * 3, out...  36.9 us

profile of v2, /device:TPU:0, one launch (start us, length us, event | category | flops | bytes accessed | tf_op | source)
XLA Modules:
  0.0 82.0 jit_solution(153126841834918591)
XLA Ops:
  0.6 44.5 %adapter_attention.1 = (bf16[128,2048]{1,0:T(8,128)(2,1)}, f32[16,8192]{1,0:T(8,128)}, f32[16,2048]{1,0:T(8,128)}) custom-call(bf16[128,8192]{1,0:T(8,128)(2,1)} %bitcast.10, bf16[128,2048]{1,0:T(8,128)(2,1)} %bitcast.11, bf16[128,256]{1,0:T(8,128)(2,1)} %bitcast.15, bf16[128,256]{1,0:T(8,128)(2,1)} %bitcast.16, bf16[128,2048]{1,0:T(8,128)(2,1)} %bitcast.12, ...), custom_call_target="tpu_custom_call" | custom-call | tf_op jit(solution)/shard_map/adapter_attention/pallas_call | solution.py:396
  45.1 36.9 %hand_over.1 = (bf16[128,2048]{1,0:T(8,128)(2,1)}, f32[16,8192]{1,0:T(8,128)}, f32[16,2048]{1,0:T(8,128)}) custom-call(bf16[128,2048]{1,0:T(8,128)(2,1)} %get-tuple-element.9.refs_0_, f32[16,8192]{1,0:T(8,128)} %get-tuple-element.10.refs_1_, f32[16,2048]{1,0:T(8,128)} %get-tuple-element.11.refs_2_), custom_call_target="tpu_custom_call" | custom-call | tf_op jit(solution)/shard_map/hand_over/pallas_call | solution.py:450

commit v3 on v2

--- a/solution.py
+++ b/solution.py
@@ -59,8 +59,10 @@
     step_down,
     step_up,
     bias,
-    scores_buf,
+    weights_buf,
     grads_buf,
+    sums_buf,
+    tops_buf,
     gbuf,
     rbuf,
     zbuf,
@@ -206,8 +208,21 @@
             kcols = pl.ds(pl.multiple_of(group * HEAD_SIZE, HEAD_SIZE), HEAD_SIZE)
             vcols = pl.ds(pl.multiple_of(kvw + group * HEAD_SIZE, HEAD_SIZE), HEAD_SIZE)
             rows = pl.ds(pl.multiple_of(group * G * BLK, G * BLK), G * BLK)
-            scores_buf[k, rows, :] = dot_nt(stacked(q, group * G, G), kv[k, :, kcols])
+            scores = dot_nt(stacked(q, group * G, G), kv[k, :, kcols])
             grads_buf[k, rows, :] = dot_nt(stacked(og, group * G, G), kv[k, :, vcols])
+            group_bias = bias[pl.ds(pl.multiple_of(group * G, G), G), k * pair : (k + 1) * pair]
+            all_weights = []
+            for j in range(G):
+                head_rows = pl.ds(pl.multiple_of((group * G + j) * BLK, BLK), BLK)
+                head_scores = scores[j * BLK : (j + 1) * BLK] * (scaling * LOG2E)
+                head_scores += group_bias[j : j + 1]
+                top = jnp.max(head_scores, axis=-1, keepdims=True)
+                tops_buf[k, head_rows, :] = jnp.broadcast_to(top, (BLK, HEAD_SIZE))
+                all_weights.append(jnp.exp2(head_scores - top).astype(BF16))
+            weights = jnp.concatenate(all_weights, axis=0)
+            weights_buf[k, rows, :] = weights
+            values = jnp.concatenate([kv[k, :, vcols], jnp.ones((pair, HEAD_SIZE), BF16)], axis=1)
+            sums_buf[k, rows, :] = dot_nn(weights, values)
             return carry
 
         lax.fori_loop(0, heads // G, group_step, 0)
@@ -223,6 +238,41 @@
         for copy in core_copies:
             copy.wait_recv()
 
+    def finish_step(i, carry):
+        first = i * per_step
+        kcols = pl.ds(pl.multiple_of(first // G * HEAD_SIZE, HEAD_SIZE), HEAD_SIZE)
+        score_grads = [[] for _ in range(nz)]
+        factors, scales = [], []
+        for j in range(per_step):
+            rows = pl.ds(pl.multiple_of((first + j) * BLK, BLK), BLK)
+            cols = pl.ds(pl.multiple_of((first + j) * HEAD_SIZE, HEAD_SIZE), HEAD_SIZE)
+            tops = [tops_buf[k, rows, :] for k in range(nz)]
+            top = functools.reduce(jnp.maximum, tops)
+            factor = [jnp.exp2(t - top) for t in tops]
+            attended, total = 0.0, 0.0
+            for k in range(nz):
+                attended += factor[k] * sums_buf[k, rows, :HEAD_SIZE]
+                total += factor[k] * sums_buf[k, rows, HEAD_SIZE:]
+            inverse = 1.0 / total
+            attended = attended * inverse
+            att[:, cols] = attended.astype(BF16)
+            inner = jnp.sum(attended * og[:, cols].astype(F32), axis=-1, keepdims=True)
+            for k in range(nz):
+                weights = weights_buf[k, rows, :].astype(F32)
+                score_grads[k].append((weights * (grads_buf[k, rows, :] - inner)).astype(BF16))
+            factors.append(factor)
+            scales.append(inverse * scaling)
+        parts = [
+            dot_nn(jnp.concatenate(score_grads[k], axis=0), kv[k, :, kcols]) for k in range(nz)
+        ]
+        for j in range(per_step):
+            cols = pl.ds(pl.multiple_of((first + j) * HEAD_SIZE, HEAD_SIZE), HEAD_SIZE)
+            query_grad = 0.0
+            for k in range(nz):
+                query_grad += factors[j][k] * parts[k][j * BLK : (j + 1) * BLK]
+            qg[:, cols] = (query_grad * scales[j]).astype(BF16)
+        return carry
+
     def head_step(i, carry):
         first = i * per_step
         group = first // G
@@ -233,14 +283,9 @@
         all_weights, all_grads, all_inverse = [], [], []
         for j in range(per_step):
             h = first + j
-            if early:
-                rows = pl.ds(pl.multiple_of(h * BLK, BLK), BLK)
-                scores = jnp.concatenate([scores_buf[k, rows, :] for k in range(nz)], axis=1)
-                weight_grad = jnp.concatenate([grads_buf[k, rows, :] for k in range(nz)], axis=1)
-            else:
-                cols = pl.ds(pl.multiple_of(h * HEAD_SIZE, HEAD_SIZE), HEAD_SIZE)
-                scores = dot_nt(q[:, cols], key_rows)
-                weight_grad = dot_nt(og[:, cols], value_rows)
+            cols = pl.ds(pl.multiple_of(h * HEAD_SIZE, HEAD_SIZE), HEAD_SIZE)
+            scores = dot_nt(q[:, cols], key_rows)
+            weight_grad = dot_nt(og[:, cols], value_rows)
             scores = scores * (scaling * LOG2E) + bias[pl.ds(h, 1), :]
             weights = jnp.exp2(scores - jnp.max(scores, axis=-1, keepdims=True))
             inverse = 1.0 / jnp.sum(weights, axis=-1, keepdims=True)
@@ -257,7 +302,7 @@
             qg[:, cols] = (query_grad[rows] * (all_inverse[j] * scaling)).astype(BF16)
         return carry
 
-    lax.fori_loop(0, heads // per_step, head_step, 0)
+    lax.fori_loop(0, heads // per_step, finish_step if early else head_step, 0)
     att_store = pltpu.make_async_copy(att, att_hbm, store_sem.at[0])
     att_store.start()
 
@@ -344,18 +389,25 @@
 
 
 def hand_over(*refs):
-    sem = refs[-1]
-    copies = []
+    sources, targets, held = refs[:3], refs[3:6], refs[6:9]
+    in_sem, out_sem = refs[9:]
+    first, second = [], []
     for i in range(3):
-        rows = refs[i].shape[0] // 2
+        rows = sources[i].shape[0] // 2
         for j in range(2):
-            part = pl.ds(j * rows, rows)
-            copies.append(
-                pltpu.make_async_copy(refs[i].at[part], refs[3 + i].at[part], sem.at[2 * i + j])
+            part, n = pl.ds(j * rows, rows), 2 * i + j
+            first.append(
+                pltpu.make_async_copy(sources[i].at[part], held[i].at[part], in_sem.at[n])
             )
-    for copy in copies:
-        copy.start()
-    for copy in copies:
+            second.append(
+                pltpu.make_async_copy(held[i].at[part], targets[i].at[part], out_sem.at[n])
+            )
+    for copy in first:
+        copy.start()
+    for arrive, leave in zip(first, second):
+        arrive.wait()
+        leave.start()
+    for copy in second:
         copy.wait()
 
 
@@ -387,7 +439,7 @@
     vmem_spec = pl.BlockSpec(memory_space=pltpu.VMEM)
     smem_spec = pl.BlockSpec(memory_space=pltpu.SMEM)
     dma = pltpu.SemaphoreType.DMA
-    held_scores = (nz, heads * tok, 2 * BLK) if early else (1, 8, 128)
+    held_rows = (nz, heads * tok) if early else (1, 16)
     results = (
         jax.ShapeDtypeStruct((tok, qw), BF16),
         jax.ShapeDtypeStruct((rank, width), F32),
@@ -409,8 +461,10 @@
             pltpu.VMEM((rank, width), F32),
             pltpu.VMEM((rank, qw), F32),
             pltpu.VMEM((heads, keys), F32),
-            pltpu.VMEM(held_scores, F32),
-            pltpu.VMEM(held_scores, F32),
+            pltpu.VMEM(held_rows + (2 * BLK,), BF16),
+            pltpu.VMEM(held_rows + (2 * BLK,), F32),
+            pltpu.VMEM(held_rows + (2 * HEAD_SIZE,), F32),
+            pltpu.VMEM(held_rows + (HEAD_SIZE,), F32),
             pltpu.VMEM((na, rank, piece), BF16),
             pltpu.VMEM((na, rank, piece), BF16),
             pltpu.VMEM((nz, rank, piece), BF16),
@@ -452,7 +506,8 @@
         out_shape=results,
         in_specs=[any_spec] * 3,
         out_specs=(any_spec,) * 3,
-        scratch_shapes=[dma((6,))],
+        scratch_shapes=[pltpu.VMEM(r.shape, r.dtype) for r in results] + [dma((6,)), dma((6,))],
+        compiler_params=pltpu.CompilerParams(vmem_limit_bytes=60 * 2**20),
         name="hand_over",
     )(*outputs)
     return attended[None], step_down.T, step_up

time: 82.2 us -> 46.1 us (0.56)
  Pallas kernels: 81.4 us -> 45.3 us
    pallas_call x1, Pallas kernels: 36.9 us -> 2.05 us  [body(): pl.pallas_call(hand_over, out_shape=results, in_specs=[any_spec] * 3, out...]
    pallas_call x1, Pallas kernels: 44.5 us -> 43.2 us  [body(): pl.pallas_call(functools.partial(kernel, ndp, nctx, per_step, early), out...]
where the time goes in v3:
time: 46.1 us; the launch traced here: 45.9 us
  Pallas kernels  45.3 us (98%)
  between operations  0.64 us (1%)
    pallas_call x1, Pallas kernels, body(): pl.pallas_call(functools.partial(kernel, ndp, nctx, per_step, early), out...  43.2 us
    pallas_call x1, Pallas kernels, body(): pl.pallas_call(hand_over, out_shape=results, in_specs=[any_spec] * 3, out...  2.05 us

profile of v3, /device:TPU:0, one launch (start us, length us, event | category | flops | bytes accessed | tf_op | source)
XLA Modules:
  0.0 45.9 jit_solution(12189355489046373062)
XLA Ops:
  0.6 43.2 %adapter_attention.1 = (bf16[128,2048]{1,0:T(8,128)(2,1)}, f32[16,8192]{1,0:T(8,128)}, f32[16,2048]{1,0:T(8,128)}) custom-call(bf16[128,8192]{1,0:T(8,128)(2,1)} %bitcast.10, bf16[128,2048]{1,0:T(8,128)(2,1)} %bitcast.11, bf16[128,256]{1,0:T(8,128)(2,1)} %bitcast.15, bf16[128,256]{1,0:T(8,128)(2,1)} %bitcast.16, bf16[128,2048]{1,0:T(8,128)(2,1)} %bitcast.12, ...), custom_call_target="tpu_custom_call" | custom-call | tf_op jit(solution)/shard_map/adapter_attention/pallas_call | solution.py:448
  43.9 2.1 %hand_over.1 = (bf16[128,2048]{1,0:T(8,128)(2,1)}, f32[16,8192]{1,0:T(8,128)}, f32[16,2048]{1,0:T(8,128)}) custom-call(bf16[128,2048]{1,0:T(8,128)(2,1)} %get-tuple-element.9.refs_0_, f32[16,8192]{1,0:T(8,128)} %get-tuple-element.10.refs_1_, f32[16,2048]{1,0:T(8,128)} %get-tuple-element.11.refs_2_), custom_call_target="tpu_custom_call" | custom-call | tf_op jit(solution)/shard_map/hand_over/pallas_call | solution.py:504

commit v4 on v3

--- a/solution.py
+++ b/solution.py
@@ -30,9 +30,23 @@
     return jnp.dot(a, b, preferred_element_type=F32)
 
 
+def send(source, target, send_sem, recv_sem, device):
+    copy = pltpu.make_async_remote_copy(
+        src_ref=source,
+        dst_ref=target,
+        send_sem=send_sem,
+        recv_sem=recv_sem,
+        device_id=device,
+        device_id_type=MESH,
+    )
+    copy.start()
+    return copy
+
+
 def kernel(
     ndp,
     nctx,
+    parts,
     per_step,
     early,
     x_hbm,
@@ -63,6 +77,8 @@
     grads_buf,
     sums_buf,
     tops_buf,
+    sbuf,
+    pbuf,
     gbuf,
     rbuf,
     zbuf,
@@ -73,17 +89,20 @@
     z_recv,
     c_send,
     c_recv,
+    p_send,
+    p_recv,
     rs_send,
     rs_recv,
     gz_send,
     gz_recv,
     ag_send,
     ag_recv,
+    af_send,
+    af_recv,
 ):
     dp, ctx = lax.axis_index("dp"), lax.axis_index("ctx")
     nz, na = nctx // 2, ndp * 2
     z, core = lax.div(ctx, 2), lax.rem(ctx, 2)
-    a = dp * 2 + core
     kvw = k_hbm.shape[1]
     width = x.shape[1]
     qw = q.shape[1]
@@ -103,9 +122,10 @@
             bit *= 2
         return other
 
+    sibling = (dp, z * 2 + 1 - core)
+
     def plane_id(k):
-        p = lax.rem(a + k, na)
-        return p, (lax.div(p, 2), z * 2 + lax.rem(p, 2))
+        return (lax.rem(dp + k, ndp), ctx)
 
     def line_id(k):
         to = lax.rem(z + k, nz) if nz & (nz - 1) else line(k)
@@ -128,41 +148,11 @@
         loads.append(copy)
 
     barrier = pltpu.get_barrier_semaphore()
-    for k in range(1, na):
-        pl.semaphore_signal(barrier, inc=1, device_id=plane_id(k)[1], device_id_type=MESH)
-    for k in range(1, nz):
-        pl.semaphore_signal(barrier, inc=1, device_id=line_id(k), device_id_type=MESH)
-    pl.semaphore_wait(barrier, na - 1 + nz - 1)
-
-    loads[0].wait()
-    loads[1].wait()
-    sibling = (dp, z * 2 + 1 - core)
-    line_copies = []
-    for k in range(1, nz):
-        copy = pltpu.make_async_remote_copy(
-            src_ref=kv.at[0, own_rows, :],
-            dst_ref=kv.at[k, own_rows, :],
-            send_sem=z_send.at[k],
-            recv_sem=z_recv.at[k],
-            device_id=line_id(k),
-            device_id_type=MESH,
-        )
-        copy.start()
-        line_copies.append(copy)
-
-    def to_sibling(k):
-        copy = pltpu.make_async_remote_copy(
-            src_ref=kv.at[k, own_rows, :],
-            dst_ref=kv.at[k, own_rows, :],
-            send_sem=c_send.at[k],
-            recv_sem=c_recv.at[k],
-            device_id=sibling,
-            device_id_type=MESH,
-        )
-        copy.start()
-        return copy
-
-    core_copies = [to_sibling(0)]
+    partners = [sibling]
+    partners += [plane_id(k) for k in range(1, ndp)]
+    partners += [line_id(k) for k in range(1, nz)]
+    for partner in partners:
+        pl.semaphore_signal(barrier, inc=1, device_id=partner, device_id_type=MESH)
 
     slots, nqb = lists.shape[:2]
     mine = lax.broadcasted_iota(jnp.int32, lists.shape, 1) == ctx
@@ -184,6 +174,21 @@
     spread = jnp.where(lax.broadcasted_iota(jnp.int32, (nqb, keys), 0) == held, 1.0, 0.0)
     count = dot_tn(count, spread)
     bias[...] = jnp.where(count > 0.5, jnp.log(jnp.maximum(count, 1.0)) * LOG2E, MASK_VALUE)
+
+    pl.semaphore_wait(barrier, len(partners))
+
+    loads[0].wait()
+    loads[1].wait()
+    line_copies = []
+    for k in range(1, nz):
+        source, target = kv.at[0, own_rows, :], kv.at[k, own_rows, :]
+        line_copies.append(send(source, target, z_send.at[k], z_recv.at[k], line_id(k)))
+
+    def to_sibling(k):
+        rows = kv.at[k, own_rows, :]
+        return send(rows, rows, c_send.at[k], c_recv.at[k], sibling)
+
+    core_copies = [to_sibling(0)]
 
     loads[2].wait()
     low_rank = dot_nt(x[...], down_t[...]).astype(BF16)
@@ -308,76 +313,82 @@
 
     low_grad = (ADAPTER_GAIN * dot_nt(qg[...], up[...])).astype(BF16)
 
-    def chunk(p):
-        dcols = pl.ds(pl.multiple_of(p * wd, 128), wd)
-        ucols = pl.ds(pl.multiple_of(p * wu, 128), wu)
-        return dot_tn(low_grad, x[:, dcols]), ADAPTER_GAIN * dot_tn(low_rank, qg[:, ucols])
-
-    rs_copies = []
-    for k in range(1, na):
-        p, device = plane_id(k)
-        part_down, part_up = chunk(p)
-        gbuf[k, :, :wd] = part_down.astype(BF16)
-        gbuf[k, :, wd:] = part_up.astype(BF16)
-        copy = pltpu.make_async_remote_copy(
-            src_ref=gbuf.at[k],
-            dst_ref=rbuf.at[k],
-            send_sem=rs_send.at[k],
-            recv_sem=rs_recv.at[k],
-            device_id=device,
-            device_id_type=MESH,
-        )
-        copy.start()
-        rs_copies.append(copy)
-    sum_down, sum_up = chunk(a)
-    for k in range(1, na):
-        rs_copies[k - 1].wait_recv()
-        sum_down += rbuf[k, :, :wd].astype(F32)
-        sum_up += rbuf[k, :, wd:].astype(F32)
-    zbuf[z, :, :wd] = sum_down.astype(BF16)
-    zbuf[z, :, wd:] = sum_up.astype(BF16)
-
-    gz_copies = []
-    for k in range(1, nz):
-        copy = pltpu.make_async_remote_copy(
-            src_ref=zbuf.at[z],
-            dst_ref=zbuf.at[z],
-            send_sem=gz_send.at[k],
-            recv_sem=gz_recv.at[k],
-            device_id=line_id(k),
-            device_id_type=MESH,
-        )
-        copy.start()
-        gz_copies.append(copy)
-    for copy in gz_copies:
-        copy.wait_recv()
-    total = zbuf[0].astype(F32)
-    for i in range(1, nz):
-        total += zbuf[i].astype(F32)
-    abuf[a] = total.astype(BF16)
-
-    ag_copies = []
-    for k in range(1, na):
-        copy = pltpu.make_async_remote_copy(
-            src_ref=abuf.at[a],
-            dst_ref=abuf.at[a],
-            send_sem=ag_send.at[k],
-            recv_sem=ag_recv.at[k],
-            device_id=plane_id(k)[1],
-            device_id_type=MESH,
-        )
-        copy.start()
-        ag_copies.append(copy)
-    for copy in line_copies + core_copies + rs_copies + gz_copies:
+    dpart, upart = wd // parts, wu // parts
+
+    def chunk(chip, part, kind):
+        p = lax.rem(dp + chip, ndp) * 2 + kind
+        dcols = pl.ds(pl.multiple_of(p * wd + part * dpart, 128), dpart)
+        ucols = pl.ds(pl.multiple_of(p * wu + part * upart, 128), upart)
+        part_down = dot_tn(low_grad, x[:, dcols])
+        part_up = ADAPTER_GAIN * dot_tn(low_rank, qg[:, ucols])
+        return jnp.concatenate([part_down, part_up], axis=1)
+
+    order = [(part, chip) for part in range(parts) for chip in list(range(1, ndp)) + [0]]
+    pair_copies, rs_copies, gz_copies, ag_copies, af_copies = {}, {}, {}, {}, {}
+    for part, chip in order:
+        n = part * ndp + chip
+        sbuf[n] = chunk(chip, part, 1 - core).astype(BF16)
+        pair_copies[n] = send(sbuf.at[n], pbuf.at[n], p_send.at[n], p_recv.at[n], sibling)
+    sums = {}
+    for part, chip in order:
+        n = part * ndp + chip
+        own = chunk(chip, part, core)
+        pair_copies[n].wait_recv()
+        own += pbuf[n].astype(F32)
+        if chip == 0:
+            sums[part] = own
+        else:
+            gbuf[n] = own.astype(BF16)
+            rs_copies[n] = send(gbuf.at[n], rbuf.at[n], rs_send.at[n], rs_recv.at[n], plane_id(chip))
+    for part in range(parts):
+        total = sums[part]
+        for chip in range(1, ndp):
+            n = part * ndp + chip
+            rs_copies[n].wait_recv()
+            total += rbuf[n].astype(F32)
+        slot = part * nz + z
+        zbuf[slot] = total.astype(BF16)
+        for k in range(1, nz):
+            n = part * nz + k
+            gz_copies[n] = send(zbuf.at[slot], zbuf.at[slot], gz_send.at[n], gz_recv.at[n], line_id(k))
+
+    def forward(part, chip):
+        n = part * ndp + chip
+        rows = abuf.at[part * na + lax.rem(dp + ndp - chip, ndp) * 2 + core]
+        return send(rows, rows, af_send.at[n], af_recv.at[n], sibling)
+
+    for part in range(parts):
+        for k in range(1, nz):
+            gz_copies[part * nz + k].wait_recv()
+        total = zbuf[part * nz].astype(F32)
+        for i in range(1, nz):
+            total += zbuf[part * nz + i].astype(F32)
+        rows = abuf.at[part * na + dp * 2 + core]
+        rows[...] = total.astype(BF16)
+        for chip in range(1, ndp):
+            n = part * ndp + chip
+            ag_copies[n] = send(rows, rows, ag_send.at[n], ag_recv.at[n], plane_id(chip))
+        af_copies[part * ndp] = forward(part, 0)
+    for part in range(parts):
+        for chip in range(1, ndp):
+            ag_copies[part * ndp + chip].wait_recv()
+            af_copies[part * ndp + chip] = forward(part, chip)
+    for copy in line_copies + core_copies:
         copy.wait_send()
+    for copies in (pair_copies, rs_copies, gz_copies, ag_copies, af_copies):
+        for copy in copies.values():
+            copy.wait_send()
     loads[5].wait()
     loads[6].wait()
-    for copy in ag_copies:
-        copy.wait()
+    for copy in af_copies.values():
+        copy.wait_recv()
     norm = (BLK * nctx * ndp) ** (-0.5)
     for p in range(na):
-        step_down[:, p * wd : (p + 1) * wd] += abuf[p, :, :wd].astype(F32) * norm
-        step_up[:, p * wu : (p + 1) * wu] += abuf[p, :, wd:].astype(F32) * norm
+        for part in range(parts):
+            total = abuf[part * na + p].astype(F32) * norm
+            dfirst, ufirst = p * wd + part * dpart, p * wu + part * upart
+            step_down[:, dfirst : dfirst + dpart] += total[:, :dpart]
+            step_up[:, ufirst : ufirst + upart] += total[:, dpart:]
     stores = [
         pltpu.make_async_copy(step_down, step_down_hbm, store_sem.at[1]),
         pltpu.make_async_copy(step_up, step_up_hbm, store_sem.at[2]),
@@ -432,7 +443,8 @@
     heads = qw // HEAD_SIZE
     keys = nctx * tok
     nz, na = nctx // 2, ndp * 2
-    piece = (width + qw) // na
+    parts = 1 if width % (256 * na) or qw % (256 * na) else 2
+    piece = (width + qw) // (na * parts)
     early = 2 * heads * tok * keys * 4 <= 2**24
     per_step = 4 if early else 1
     any_spec = pl.BlockSpec(memory_space=pl.ANY)
@@ -446,7 +458,7 @@
         jax.ShapeDtypeStruct((rank, qw), F32),
     )
     outputs = pl.pallas_call(
-        functools.partial(kernel, ndp, nctx, per_step, early),
+        functools.partial(kernel, ndp, nctx, parts, per_step, early),
         out_shape=results,
         in_specs=[any_spec] * 7 + [vmem_spec] * 3 + [smem_spec],
         out_specs=(any_spec,) * 3,
@@ -465,22 +477,28 @@
             pltpu.VMEM(held_rows + (2 * BLK,), F32),
             pltpu.VMEM(held_rows + (2 * HEAD_SIZE,), F32),
             pltpu.VMEM(held_rows + (HEAD_SIZE,), F32),
-            pltpu.VMEM((na, rank, piece), BF16),
-            pltpu.VMEM((na, rank, piece), BF16),
-            pltpu.VMEM((nz, rank, piece), BF16),
-            pltpu.VMEM((na, rank, piece), BF16),
+            pltpu.VMEM((parts * ndp, rank, piece), BF16),
+            pltpu.VMEM((parts * ndp, rank, piece), BF16),
+            pltpu.VMEM((parts * ndp, rank, piece), BF16),
+            pltpu.VMEM((parts * ndp, rank, piece), BF16),
+            pltpu.VMEM((parts * nz, rank, piece), BF16),
+            pltpu.VMEM((parts * na, rank, piece), BF16),
             dma((7,)),
             dma((3,)),
             dma((nz,)),
             dma((nz,)),
             dma((nz,)),
             dma((nz,)),
-            dma((na,)),
-            dma((na,)),
-            dma((nz,)),
-            dma((nz,)),
-            dma((na,)),
-            dma((na,)),
+            dma((parts * ndp,)),
+            dma((parts * ndp,)),
+            dma((parts * ndp,)),
+            dma((parts * ndp,)),
+            dma((parts * nz,)),
+            dma((parts * nz,)),
+            dma((parts * ndp,)),
+            dma((parts * ndp,)),
+            dma((parts * ndp,)),
+            dma((parts * ndp,)),
         ],
         compiler_params=pltpu.CompilerParams(
             collective_id=0,

time: 46.1 us -> 44.6 us (0.967)
  Pallas kernels: 45.3 us -> 43.8 us
    pallas_call x1, Pallas kernels: 43.2 us -> 41.7 us  [body(): pl.pallas_call(functools.partial(kernel, ndp, nctx, parts, per_step, earl...]
where the time goes in v4:
time: 44.6 us; the launch traced here: 44.4 us
  Pallas kernels  43.8 us (98%)
  between operations  0.64 us (1%)
    pallas_call x1, Pallas kernels, body(): pl.pallas_call(functools.partial(kernel, ndp, nctx, parts, per_step, earl...  41.7 us
    pallas_call x1, Pallas kernels, body(): pl.pallas_call(hand_over, out_shape=results, in_specs=[any_spec] * 3, out...  2.05 us

profile of v4, /device:TPU:0, one launch (start us, length us, event | category | flops | bytes accessed | tf_op | source)
XLA Modules:
  0.0 44.4 jit_solution(12543163030334730791)
XLA Ops:
  0.6 41.7 %adapter_attention.1 = (bf16[128,2048]{1,0:T(8,128)(2,1)}, f32[16,8192]{1,0:T(8,128)}, f32[16,2048]{1,0:T(8,128)}) custom-call(bf16[128,8192]{1,0:T(8,128)(2,1)} %bitcast.10, bf16[128,2048]{1,0:T(8,128)(2,1)} %bitcast.11, bf16[128,256]{1,0:T(8,128)(2,1)} %bitcast.15, bf16[128,256]{1,0:T(8,128)(2,1)} %bitcast.16, bf16[128,2048]{1,0:T(8,128)(2,1)} %bitcast.12, ...), custom_call_target="tpu_custom_call" | custom-call | tf_op jit(solution)/shard_map/adapter_attention/pallas_call | solution.py:460
  42.3 2.1 %hand_over.1 = (bf16[128,2048]{1,0:T(8,128)(2,1)}, f32[16,8192]{1,0:T(8,128)}, f32[16,2048]{1,0:T(8,128)}) custom-call(bf16[128,2048]{1,0:T(8,128)(2,1)} %get-tuple-element.9.refs_0_, f32[16,8192]{1,0:T(8,128)} %get-tuple-element.10.refs_1_, f32[16,2048]{1,0:T(8,128)} %get-tuple-element.11.refs_2_), custom_call_target="tpu_custom_call" | custom-call | tf_op jit(solution)/shard_map/hand_over/pallas_call | solution.py:522

commit v5 on v4

--- a/solution.py
+++ b/solution.py
@@ -77,6 +77,7 @@
     grads_buf,
     sums_buf,
     tops_buf,
+    gown,
     sbuf,
     pbuf,
     gbuf,
@@ -192,6 +193,9 @@
 
     loads[2].wait()
     low_rank = dot_nt(x[...], down_t[...]).astype(BF16)
+    tok_iota = [lax.broadcasted_iota(jnp.int32, (BLK, BLK), i) for i in range(2)]
+    identity = jnp.where(tok_iota[0] == tok_iota[1], 1.0, 0.0).astype(BF16)
+    low_rank_t = dot_tn(low_rank, identity).astype(BF16)
     loads[3].wait()
     q[...] = (frozen[...].astype(F32) + ADAPTER_GAIN * dot_nn(low_rank, up[...])).astype(BF16)
 
@@ -311,28 +315,31 @@
     att_store = pltpu.make_async_copy(att, att_hbm, store_sem.at[0])
     att_store.start()
 
-    low_grad = (ADAPTER_GAIN * dot_nt(qg[...], up[...])).astype(BF16)
+    low_grad_t = (ADAPTER_GAIN * dot_nt(up[...], qg[...])).astype(BF16)
 
     dpart, upart = wd // parts, wu // parts
 
-    def chunk(chip, part, kind):
-        p = lax.rem(dp + chip, ndp) * 2 + kind
-        dcols = pl.ds(pl.multiple_of(p * wd + part * dpart, 128), dpart)
-        ucols = pl.ds(pl.multiple_of(p * wu + part * upart, 128), upart)
-        part_down = dot_tn(low_grad, x[:, dcols])
-        part_up = ADAPTER_GAIN * dot_tn(low_rank, qg[:, ucols])
-        return jnp.concatenate([part_down, part_up], axis=1)
+    def owner(chip, kind):
+        return lax.rem(dp + chip, ndp) * 2 + kind
 
     order = [(part, chip) for part in range(parts) for chip in list(range(1, ndp)) + [0]]
     pair_copies, rs_copies, gz_copies, ag_copies, af_copies = {}, {}, {}, {}, {}
-    for part, chip in order:
-        n = part * ndp + chip
-        sbuf[n] = chunk(chip, part, 1 - core).astype(BF16)
-        pair_copies[n] = send(sbuf.at[n], pbuf.at[n], p_send.at[n], p_recv.at[n], sibling)
+    for part in range(parts):
+        for p in range(na):
+            dfirst, ufirst = p * wd + part * dpart, p * wu + part * upart
+            part_down = dot_nn(low_grad_t, x[:, dfirst : dfirst + dpart])
+            part_up = ADAPTER_GAIN * dot_nn(low_rank_t, qg[:, ufirst : ufirst + upart])
+            both = jnp.concatenate([part_down, part_up], axis=1)
+            gown[part * na + p] = both
+            sbuf[part * na + p] = both.astype(BF16)
+        for chip in list(range(1, ndp)) + [0]:
+            n = part * ndp + chip
+            source = sbuf.at[part * na + owner(chip, 1 - core)]
+            pair_copies[n] = send(source, pbuf.at[n], p_send.at[n], p_recv.at[n], sibling)
     sums = {}
     for part, chip in order:
         n = part * ndp + chip
-        own = chunk(chip, part, core)
+        own = gown[part * na + owner(chip, core)]
         pair_copies[n].wait_recv()
         own += pbuf[n].astype(F32)
         if chip == 0:
@@ -477,7 +484,8 @@
             pltpu.VMEM(held_rows + (2 * BLK,), F32),
             pltpu.VMEM(held_rows + (2 * HEAD_SIZE,), F32),
             pltpu.VMEM(held_rows + (HEAD_SIZE,), F32),
-            pltpu.VMEM((parts * ndp, rank, piece), BF16),
+            pltpu.VMEM((parts * na, rank, piece), F32),
+            pltpu.VMEM((parts * na, rank, piece), BF16),
             pltpu.VMEM((parts * ndp, rank, piece), BF16),
             pltpu.VMEM((parts * ndp, rank, piece), BF16),
             pltpu.VMEM((parts * ndp, rank, piece), BF16),

time: 44.6 us -> 44.7 us (level)
  no operation moved by 1% of the time
where the time goes in v5:
time: 44.7 us; the launch traced here: 44.5 us
  Pallas kernels  43.9 us (98%)
  between operations  0.64 us (1%)
    pallas_call x1, Pallas kernels, body(): pl.pallas_call(functools.partial(kernel, ndp, nctx, parts, per_step, earl...  41.8 us
    pallas_call x1, Pallas kernels, body(): pl.pallas_call(hand_over, out_shape=results, in_specs=[any_spec] * 3, out...  2.05 us

profile of v5, /device:TPU:0, one launch (start us, length us, event | category | flops | bytes accessed | tf_op | source)
XLA Modules:
  0.0 44.5 jit_solution(16724509683027774214)
XLA Ops:
  0.6 41.8 %adapter_attention.1 = (bf16[128,2048]{1,0:T(8,128)(2,1)}, f32[16,8192]{1,0:T(8,128)}, f32[16,2048]{1,0:T(8,128)}) custom-call(bf16[128,8192]{1,0:T(8,128)(2,1)} %bitcast.10, bf16[128,2048]{1,0:T(8,128)(2,1)} %bitcast.11, bf16[128,256]{1,0:T(8,128)(2,1)} %bitcast.15, bf16[128,256]{1,0:T(8,128)(2,1)} %bitcast.16, bf16[128,2048]{1,0:T(8,128)(2,1)} %bitcast.12, ...), custom_call_target="tpu_custom_call" | custom-call | tf_op jit(solution)/shard_map/adapter_attention/pallas_call | solution.py:467
  42.5 2.1 %hand_over.1 = (bf16[128,2048]{1,0:T(8,128)(2,1)}, f32[16,8192]{1,0:T(8,128)}, f32[16,2048]{1,0:T(8,128)}) custom-call(bf16[128,2048]{1,0:T(8,128)(2,1)} %get-tuple-element.9.refs_0_, f32[16,8192]{1,0:T(8,128)} %get-tuple-element.10.refs_1_, f32[16,2048]{1,0:T(8,128)} %get-tuple-element.11.refs_2_), custom_call_target="tpu_custom_call" | custom-call | tf_op jit(solution)/shard_map/hand_over/pallas_call | solution.py:530

commit v6 on v5

--- a/solution.py
+++ b/solution.py
@@ -30,8 +30,8 @@
     return jnp.dot(a, b, preferred_element_type=F32)
 
 
-def send(source, target, send_sem, recv_sem, device):
-    copy = pltpu.make_async_remote_copy(
+def remote(source, target, send_sem, recv_sem, device):
+    return pltpu.make_async_remote_copy(
         src_ref=source,
         dst_ref=target,
         send_sem=send_sem,
@@ -39,6 +39,10 @@
         device_id=device,
         device_id_type=MESH,
     )
+
+
+def send(*ends):
+    copy = remote(*ends)
     copy.start()
     return copy
 
@@ -183,7 +187,17 @@
     line_copies = []
     for k in range(1, nz):
         source, target = kv.at[0, own_rows, :], kv.at[k, own_rows, :]
-        line_copies.append(send(source, target, z_send.at[k], z_recv.at[k], line_id(k)))
+        line_copies.append(
+            remote(source, target, z_send.at[k], z_recv.at[k], line_id(k))
+        )
+    staged = nz == 4
+    middle = (z == 1) | (z == 2)
+    line_copies[0].start()
+    if staged:
+        pl.when(middle)(line_copies[2].start)
+    else:
+        for copy in line_copies[1:]:
+            copy.start()
 
     def to_sibling(k):
         rows = kv.at[k, own_rows, :]
@@ -193,6 +207,8 @@
 
     loads[2].wait()
     low_rank = dot_nt(x[...], down_t[...]).astype(BF16)
+    if staged:
+        line_copies[1].start()
     tok_iota = [lax.broadcasted_iota(jnp.int32, (BLK, BLK), i) for i in range(2)]
     identity = jnp.where(tok_iota[0] == tok_iota[1], 1.0, 0.0).astype(BF16)
     low_rank_t = dot_tn(low_rank, identity).astype(BF16)
@@ -243,6 +259,8 @@
         if early:
             core_copies[k].wait_recv()
             scores_of(k)
+        if staged and k == 0:
+            pl.when(jnp.logical_not(middle))(line_copies[2].start)
     if not early:
         for copy in core_copies:
             copy.wait_recv()

time: 44.7 us -> 46.4 us (1.038)
  Pallas kernels: 43.9 us -> 45.6 us
    pallas_call x1, Pallas kernels: 41.8 us -> 43.5 us  [body(): pl.pallas_call(functools.partial(kernel, ndp, nctx, parts, per_step, earl...]
where the time goes in v6:
time: 46.4 us; the launch traced here: 46.2 us
  Pallas kernels  45.6 us (98%)
  between operations  0.64 us (1%)
    pallas_call x1, Pallas kernels, body(): pl.pallas_call(functools.partial(kernel, ndp, nctx, parts, per_step, earl...  43.5 us
    pallas_call x1, Pallas kernels, body(): pl.pallas_call(hand_over, out_shape=results, in_specs=[any_spec] * 3, out...  2.05 us

profile of v6, /device:TPU:0, one launch (start us, length us, event | category | flops | bytes accessed | tf_op | source)
XLA Modules:
  0.0 46.2 jit_solution(1691513192511541228)
XLA Ops:
  0.6 43.5 %adapter_attention.1 = (bf16[128,2048]{1,0:T(8,128)(2,1)}, f32[16,8192]{1,0:T(8,128)}, f32[16,2048]{1,0:T(8,128)}) custom-call(bf16[128,8192]{1,0:T(8,128)(2,1)} %bitcast.10, bf16[128,2048]{1,0:T(8,128)(2,1)} %bitcast.11, bf16[128,256]{1,0:T(8,128)(2,1)} %bitcast.15, bf16[128,256]{1,0:T(8,128)(2,1)} %bitcast.16, bf16[128,2048]{1,0:T(8,128)(2,1)} %bitcast.12, ...), custom_call_target="tpu_custom_call" | custom-call | tf_op jit(solution)/shard_map/adapter_attention/pallas_call | solution.py:485
  44.1 2.1 %hand_over.1 = (bf16[128,2048]{1,0:T(8,128)(2,1)}, f32[16,8192]{1,0:T(8,128)}, f32[16,2048]{1,0:T(8,128)}) custom-call(bf16[128,2048]{1,0:T(8,128)(2,1)} %get-tuple-element.9.refs_0_, f32[16,8192]{1,0:T(8,128)} %get-tuple-element.10.refs_1_, f32[16,2048]{1,0:T(8,128)} %get-tuple-element.11.refs_2_), custom_call_target="tpu_custom_call" | custom-call | tf_op jit(solution)/shard_map/hand_over/pallas_call | solution.py:548

commit v7 on v4

--- a/solution.py
+++ b/solution.py
@@ -154,6 +154,23 @@
     for partner in partners:
         pl.semaphore_signal(barrier, inc=1, device_id=partner, device_id_type=MESH)
 
+    pl.semaphore_wait(barrier, len(partners))
+
+    line_copies = []
+    for k in range(1, nz):
+        for i, source in enumerate((k_hbm, v_hbm)):
+            target = kv.at[k, own_rows, pl.ds(i * kvw, kvw)]
+            n = i * nz + k
+            line_copies.append(send(source, target, z_send.at[n], z_recv.at[n], line_id(k)))
+
+    def to_sibling(k):
+        rows = kv.at[k, own_rows, :]
+        return send(rows, rows, c_send.at[k], c_recv.at[k], sibling)
+
+    loads[0].wait()
+    loads[1].wait()
+    core_copies = [to_sibling(0)]
+
     slots, nqb = lists.shape[:2]
     mine = lax.broadcasted_iota(jnp.int32, lists.shape, 1) == ctx
     local = jnp.sum(jnp.where(mine, lists[...].astype(F32), 0.0), axis=1)
@@ -174,21 +191,6 @@
     spread = jnp.where(lax.broadcasted_iota(jnp.int32, (nqb, keys), 0) == held, 1.0, 0.0)
     count = dot_tn(count, spread)
     bias[...] = jnp.where(count > 0.5, jnp.log(jnp.maximum(count, 1.0)) * LOG2E, MASK_VALUE)
-
-    pl.semaphore_wait(barrier, len(partners))
-
-    loads[0].wait()
-    loads[1].wait()
-    line_copies = []
-    for k in range(1, nz):
-        source, target = kv.at[0, own_rows, :], kv.at[k, own_rows, :]
-        line_copies.append(send(source, target, z_send.at[k], z_recv.at[k], line_id(k)))
-
-    def to_sibling(k):
-        rows = kv.at[k, own_rows, :]
-        return send(rows, rows, c_send.at[k], c_recv.at[k], sibling)
-
-    core_copies = [to_sibling(0)]
 
     loads[2].wait()
     low_rank = dot_nt(x[...], down_t[...]).astype(BF16)
@@ -234,7 +236,8 @@
 
     for k in range(nz):
         if k > 0:
-            line_copies[k - 1].wait_recv()
+            for copy in line_copies[2 * k - 2 : 2 * k]:
+                copy.wait_recv()
             core_copies.append(to_sibling(k))
         if early:
             core_copies[k].wait_recv()
@@ -485,8 +488,8 @@
             pltpu.VMEM((parts * na, rank, piece), BF16),
             dma((7,)),
             dma((3,)),
-            dma((nz,)),
-            dma((nz,)),
+            dma((2 * nz,)),
+            dma((2 * nz,)),
             dma((nz,)),
             dma((nz,)),
             dma((parts * ndp,)),

time: 44.6 us -> 44.9 us (level)
  no operation moved by 1% of the time
where the time goes in v7:
time: 44.9 us; the launch traced here: 44.7 us
  Pallas kernels  44.1 us (98%)
  between operations  0.64 us (1%)
    pallas_call x1, Pallas kernels, body(): pl.pallas_call(functools.partial(kernel, ndp, nctx, parts, per_step, earl...  42 us
    pallas_call x1, Pallas kernels, body(): pl.pallas_call(hand_over, out_shape=results, in_specs=[any_spec] * 3, out...  2.05 us

profile of v7, /device:TPU:0, one launch (start us, length us, event | category | flops | bytes accessed | tf_op | source)
XLA Modules:
  0.0 44.7 jit_solution(3560849236791179407)
XLA Ops:
  0.6 42.0 %adapter_attention.1 = (bf16[128,2048]{1,0:T(8,128)(2,1)}, f32[16,8192]{1,0:T(8,128)}, f32[16,2048]{1,0:T(8,128)}) custom-call(bf16[128,8192]{1,0:T(8,128)(2,1)} %bitcast.10, bf16[128,2048]{1,0:T(8,128)(2,1)} %bitcast.11, bf16[128,256]{1,0:T(8,128)(2,1)} %bitcast.15, bf16[128,256]{1,0:T(8,128)(2,1)} %bitcast.16, bf16[128,2048]{1,0:T(8,128)(2,1)} %bitcast.12, ...), custom_call_target="tpu_custom_call" | custom-call | tf_op jit(solution)/shard_map/adapter_attention/pallas_call | solution.py:463
  42.7 2.1 %hand_over.1 = (bf16[128,2048]{1,0:T(8,128)(2,1)}, f32[16,8192]{1,0:T(8,128)}, f32[16,2048]{1,0:T(8,128)}) custom-call(bf16[128,2048]{1,0:T(8,128)(2,1)} %get-tuple-element.9.refs_0_, f32[16,8192]{1,0:T(8,128)} %get-tuple-element.10.refs_1_, f32[16,2048]{1,0:T(8,128)} %get-tuple-element.11.refs_2_), custom_call_target="tpu_custom_call" | custom-call | tf_op jit(solution)/shard_map/hand_over/pallas_call | solution.py:525
